TPU v7x, 128 devices: a whole 4x4x4 slice. The times are simulated.
128 devices in a mesh: space: 16 (over y, z), grp: 8 (over x, core).
Axes of the slice: x: 4, y: 4, z: 4, core: 2. Of those that a mesh axis runs over, the one named last changes fastest.
Arguments:
- rel_vec: float32 [3, 262144], P(None, ('space', 'grp'))
- atom_feat: bfloat16 [32768, 256], P(('space', 'grp')), may hold values from -6 to 6
- centre: int32 [262144], P(('space', 'grp')), may hold values from 0 to 255
- nbr_slot: int32 [262144], P(('space', 'grp')), may hold values from 0 to 1279, as said below
- edge_mask: int32 [262144], P(('space', 'grp')), may hold values from 0 to 1, as said below
- send_rows: int32 [128, 128], P(('space', 'grp')), may hold values from 0 to 255, as said below
- w_radial: float32 [8, 256], replicated, may hold values from -2 to 2
- w_centre: bfloat16 [256, 256], replicated, may hold values from -0.375 to 0.375
- w_nbr: bfloat16 [256, 256], replicated, may hold values from -0.375 to 0.375
- w_env: bfloat16 [256, 64], replicated, may hold values from -0.375 to 0.375
- w_val: bfloat16 [256, 64], replicated, may hold values from -0.375 to 0.375
- w_mix: bfloat16 [256, 256], replicated, may hold values from -0.375 to 0.375
- w_scal: bfloat16 [192, 256], replicated, may hold values from -0.4375 to 0.4375
- w_read: bfloat16 [256, 256], replicated, may hold values from -0.375 to 0.375
- w_out: float32 [256], replicated, may hold values from -0.375 to 0.375
Outputs:
- atom_energy: float32 [32768], P(('space', 'grp'))
- forces: float32 [3, 32768], P(None, ('space', 'grp'))
Inputs may be any that keep to these rules, and one draw needn't show every extreme that they name: `nbr_slot`: every row of a device's table, 256 own rows and 1024 received ones, is named by at least one edge of that device. `edge_mask`: within each aligned block of 128 edges the real edges form a leading run; some blocks are empty, and how many differs from device to device. `send_rows`: the 128 atoms of one device's list are distinct.
All inputs are finite; a program needn't handle non-finite values.
Results may differ from a plain program's by a relative error of at most 0.015.
Values may be sent and summed in bfloat16 or wider, within the bound.
A program may use at most 64 MiB of HBM per device.

v0:
```python
import math

import jax
import jax.numpy as jnp
from jax import lax
from jax.sharding import PartitionSpec as P


def padded_2(cells, sides, width):
    for axis, dim in sides:
        count = lax.axis_size(axis)
        head = lax.slice_in_dim(cells, 0, width, axis=dim)
        tail = lax.slice_in_dim(cells, cells.shape[dim] - width, cells.shape[dim], axis=dim)
        cells = jnp.concatenate(
            [
                lax.ppermute(tail, axis, [(i, (i + 1) % count) for i in range(count)]),
                cells,
                lax.ppermute(head, axis, [((i + 1) % count, i) for i in range(count)]),
            ],
            axis=dim,
        )
    return cells


def harmonics(unit):
    xs, ys, zs = (unit[0], unit[1], unit[2])
    root3 = math.sqrt(3.0)
    root15 = math.sqrt(15.0)
    root5 = math.sqrt(5.0)
    return jnp.stack(
        [
            jnp.ones_like(xs),
            root3 * xs,
            root3 * ys,
            root3 * zs,
            root15 * xs * ys,
            root15 * ys * zs,
            0.5 * root5 * (3.0 * zs * zs - 1.0),
            root15 * xs * zs,
            0.5 * root15 * (xs * xs - ys * ys),
        ],
        axis=0,
    )


def edge_energies(
    vec, pre, centre, maskf, atoms, w_radial, w_env, w_val, w_mix, w_scal, w_read, w_out
):
    cutoff = 5.0
    count = vec.shape[1]
    dist = jnp.sqrt(jnp.sum(vec * vec, axis=0))
    harm = harmonics(vec / dist[None, :])
    ratio = dist / cutoff
    envelope = 1.0 - 28.0 * ratio**6 + 48.0 * ratio**7 - 21.0 * ratio**8
    orders = jnp.arange(1, w_radial.shape[0] + 1).astype(jnp.float32)
    radial = (
        math.sqrt(2.0 / cutoff)
        * jnp.sin(orders[:, None] * math.pi * ratio[None, :])
        / dist[None, :]
    )
    lifted = jnp.dot(radial.T, w_radial, precision=lax.Precision.HIGHEST) + pre
    latent = (jax.nn.silu(lifted) * envelope[:, None]).astype(jnp.bfloat16)
    weights = jnp.dot(latent, w_env, preferred_element_type=jnp.float32) * maskf[:, None]
    values = jnp.dot(latent, w_val, preferred_element_type=jnp.float32)
    chan = w_env.shape[1]
    spread = (harm.T[:, :, None] * weights[:, None, :]).reshape(count, 9 * chan)
    env = jax.ops.segment_sum(spread, centre, num_segments=atoms) * 0.125
    local = env[centre].reshape(count, 9, chan) * harm.T[:, :, None]
    scal = jnp.concatenate(
        [
            local[:, 0] * values,
            jnp.sum(local[:, 1:4], axis=1) * values,
            jnp.sum(local[:, 4:9], axis=1) * values,
        ],
        axis=1,
    ).astype(jnp.bfloat16)
    update = jnp.dot(latent, w_mix, preferred_element_type=jnp.float32) + jnp.dot(
        scal, w_scal, preferred_element_type=jnp.float32
    )
    mixed = (latent.astype(jnp.float32) + jax.nn.silu(update)).astype(jnp.bfloat16)
    hidden = jax.nn.silu(jnp.dot(mixed, w_read, preferred_element_type=jnp.float32))
    energy = jnp.sum(hidden * w_out[None, :], axis=1) * maskf
    return jax.ops.segment_sum(energy, centre, num_segments=atoms)


def per_device(
    rel_vec,
    atom_feat,
    centre,
    nbr_slot,
    edge_mask,
    send_rows,
    w_radial,
    w_centre,
    w_nbr,
    w_env,
    w_val,
    w_mix,
    w_scal,
    w_read,
    w_out,
):
    slots = send_rows.shape[1]
    atoms = atom_feat.shape[0]
    width = atom_feat.shape[1]
    own_list = send_rows[0]
    outgoing = atom_feat[own_list].reshape(1, 1, slots, width)
    padded = padded_2(outgoing, (("space", 0), ("grp", 1)), 1)
    flat = padded.reshape(9, slots, width)
    remote = jnp.concatenate([flat[:4], flat[5:]], axis=0).reshape(8 * slots, width)
    table = jnp.concatenate([atom_feat, remote], axis=0)
    centre_proj = jnp.dot(atom_feat, w_centre, preferred_element_type=jnp.float32)
    table_proj = jnp.dot(table, w_nbr, preferred_element_type=jnp.float32)
    pre = centre_proj[centre] + table_proj[nbr_slot]
    maskf = edge_mask.astype(jnp.float32)

    def energy_of(vectors):
        return edge_energies(
            vectors, pre, centre, maskf, atoms, w_radial, w_env, w_val, w_mix, w_scal, w_read, w_out
        )

    energies, pull = jax.vjp(energy_of, rel_vec)
    grad = pull(jnp.ones_like(energies))[0]
    centre_force = jax.ops.segment_sum(grad.T, centre, num_segments=atoms).T
    table_sums = jax.ops.segment_sum(grad.T, nbr_slot, num_segments=atoms + 8 * slots)
    own_part = table_sums[:atoms].T
    remote_sums = table_sums[atoms:].reshape(8, slots, 3)
    blank = jnp.zeros((1, slots, 3), jnp.float32)
    cell_sums = jnp.concatenate([remote_sums[:4], blank, remote_sums[4:]], axis=0)
    cell_sums = jnp.transpose(cell_sums, (0, 2, 1)).reshape(3, 3, 3, slots)
    back = padded_2(cell_sums, (("space", 0), ("grp", 1)), 1)
    returned = (
        back[0, 0]
        + back[0, 2]
        + back[0, 4]
        + back[2, 0]
        + back[2, 2]
        + back[2, 4]
        + back[4, 0]
        + back[4, 2]
        + back[4, 4]
    )
    away = jax.ops.segment_sum(returned.T, own_list, num_segments=atoms).T
    return (energies, centre_force - own_part - away)


def solution(mesh):
    placed = (
        P(None, ("space", "grp")),
        P(("space", "grp"), None),
        P(("space", "grp")),
        P(("space", "grp")),
        P(("space", "grp")),
        P(("space", "grp"), None),
        P(),
        P(),
        P(),
        P(),
        P(),
        P(),
        P(),
        P(),
        P(),
    )
    return jax.shard_map(
        per_device,
        mesh=mesh,
        in_specs=placed,
        out_specs=(P(("space", "grp")), P(None, ("space", "grp"))),
        check_vma=False,
    )
```

profile of v0, /device:TPU:1, one launch (start us, length us, event | category | flops | bytes accessed | tf_op | source)
XLA Modules:
  0.0 221.6 jit_solution(15131418801740764378)
XLA Ops:
  3.0 7.1 %collective-permute-start.1 = (bf16[1,1,128,256]{3,2,1,0:T(8,128)(2,1)S(1)}, bf16[1,1,128,256]{3,2,1,0:T(8,128)(2,1)S(1)}, u32[]{:S(2)}, u32[]{:S(2)}) collective-permute-start(bf16[1,1,128,256]{3,2,1,0:T(8,128)(2,1)S(1)} %bitcast.80), channel_id=1, source_target_pairs={{8,0},{16,8},{24,16},{32,24},{40,32},{48,40},{56,48},{64,56},{72,6... | collective-permute-start | bytes 196616 | tf_op jit(solution)/shard_map/ppermute | solution.py:18
  15.6 6.6 %gather_fusion = f32[2048,256]{1,0:T(8,128)S(1)} fusion(f32[256,256]{1,0:T(8,128)S(1)} %fusion.109, s32[2048]{0:T(1024)S(1)} %get-tuple-element.47), kind=kCustom, calls=%fused_computation | custom fusion | bytes 4202496 | tf_op jit(solution)/shard_map/gather | solution.py:114
  24.7 22.0 %gather_fusion.4 = f32[2048]{0:T(1024)} fusion(f32[256]{0:T(256)S(1)} %broadcast_in_dim.69, s32[2048]{0:T(1024)S(1)} %get-tuple-element.48), kind=kCustom, calls=%fused_computation.4 | custom fusion | bytes 24576 | tf_op jit(solution)/shard_map/transpose(jvp())/gather | solution.py:83
  51.4 2.7 %collective-permute-done.3 = bf16[3,1,128,256]{3,2,1,0:T(8,128)(2,1)S(1)} collective-permute-done((bf16[3,1,128,256]{3,2,1,0:T(8,128)(2,1)S(1)}, bf16[3,1,128,256]{3,2,1,0:T(8,128)(2,1)S(1)}, u32[]{:S(2)}, u32[]{:S(2)}) %collective-permute-start.3) | collective-permute-done | bytes 196640 | tf_op jit(solution)/shard_map/ppermute | solution.py:18
  54.7 7.6 %gather_fusion.2 = f32[2048,256]{1,0:T(8,128)S(1)} fusion(f32[1280,256]{1,0:T(8,128)S(1)} %fusion.31, s32[2048]{0:T(1024)} %fusion.86), kind=kCustom, calls=%fused_computation.2 | custom fusion | bytes 4202496 | tf_op jit(solution)/shard_map/gather | solution.py:114
  64.2 6.1 %multiply_convert_fusion = (bf16[2048,256]{0,1:T(8,128)(2,1)S(1)}, f32[2048,256]{0,1:T(8,128)}) fusion(f32[2048]{0:T(1024)S(1)} %copy-done.29, f32[2048,256]{0,1:T(8,128)} %copy.39, f32[2048,256]{0,1:T(8,128)} %copy.40, f32[8,256]{1,0:T(8,128)S(1)} %copy-done.33, f32[2048]{0:T(1024)S(1)} %copy-done.19, f32[2048]{0:T(1024)S(1)} %copy-done.27, ...), kind=kOutput, calls=%fused_computation.55 | convolution fusion | flops 54575104 | bytes 7372832 | tf_op jit(solution)/shard_map/jvp()/dot_general | solution.py:61
  70.6 2.8 %broadcast_multiply_fusion = f32[2048,9,64]{0,2,1:T(8,128)} fusion(f32[2048,64]{0,1:T(8,128)S(1)} %convolution_multiply_fusion, f32[2048,9]{0,1:T(8,128)S(1)} %bitcast.72), kind=kLoop, calls=%fused_computation.40 | loop fusion | flops 1179648 | bytes 5316608 | tf_op jit(solution)/shard_map/jvp()/mul | solution.py:66
  73.4 5.8 %copy.41 = f32[2048,576]{1,0:T(8,128)} copy(f32[2048,576]{0,1:T(8,128)} %bitcast.71) | data formatting | bytes 9437184 | tf_op jit(solution)/shard_map/jvp()/mul | solution.py:66
  79.2 14.7 %scatter_custom_fusion = f32[256,576]{1,0:T(8,128)S(1)} fusion(s32[2048]{0:T(1024)S(1)} %copy-done.25, f32[2048,576]{1,0:T(8,128)} %copy.41, f32[]{:T(128)} %constant.24.clone.1), kind=kCustom, calls=%fused_computation.98 | custom fusion | flops 1179648 | bytes 590336 | tf_op jit(solution)/shard_map/jvp()/scatter-add | solution.py:67
  94.0 9.3 %gather_fusion.3 = f32[2048,576]{1,0:T(8,128)} fusion(f32[256,576]{1,0:T(8,128)S(1)} %broadcast_multiply_fusion.3, s32[2048]{0:T(1024)S(1)} %get-tuple-element.47), kind=kCustom, calls=%fused_computation.3 | custom fusion | bytes 9445376 | tf_op jit(solution)/shard_map/jvp()/gather | solution.py:68
  103.3 5.8 %copy.42 = f32[2048,576]{0,1:T(8,128)} copy(f32[2048,576]{1,0:T(8,128)} %gather_fusion.3) | data formatting | bytes 9437184 | tf_op jit(solution)/shard_map/jvp()/gather | solution.py:68
  109.1 2.8 %broadcast_multiply_fusion.1 = f32[2048,9,64]{0,2,1:T(8,128)S(1)} fusion(f32[2048,9,64]{0,2,1:T(8,128)} %bitcast.65, f32[2048,9]{0,1:T(8,128)S(1)} %bitcast.73), kind=kLoop, calls=%fused_computation.41 | loop fusion | flops 1179648 | bytes 9510912 | tf_op jit(solution)/shard_map/jvp()/mul | solution.py:68
  121.1 2.8 %fusion = (f32[2048,9,64]{0,2,1:T(8,128)}, f32[2048,9]{0,1:T(8,128)S(1)}) fusion(f32[2048,1,64]{0,2,1:T(8,128)S(1)} %get-tuple-element.17, f32[2048,3,64]{0,2,1:T(8,128)S(1)} %broadcast_in_dim.73, f32[2048,5,64]{0,2,1:T(8,128)S(1)} %broadcast_in_dim.72, f32[2048,9]{0,1:T(8,128)S(1)} %bitcast.74, f32[2048,9,64]{0,2,1:T(8,128)S(1)} %bitcast.68), kind=kLoop, calls=%fused_computation.16 | loop fusion | flops 5879808 | bytes 14303232 | tf_op jit(solution)/shard_map/transpose(jvp())/mul | solution.py:68
  123.9 5.8 %copy.45 = f32[2048,576]{1,0:T(8,128)} copy(f32[2048,576]{0,1:T(8,128)} %bitcast.69) | data formatting | bytes 9437184 | tf_op jit(solution)/shard_map/transpose(jvp())/reshape | solution.py:68
  129.7 14.8 %scatter_custom_fusion.2 = f32[256,576]{1,0:T(8,128)S(1)} fusion(s32[2048]{0:T(1024)} %get-tuple-element.46, f32[2048,576]{1,0:T(8,128)} %copy.45, f32[]{:T(128)} %constant.24.clone.1), kind=kCustom, calls=%fused_computation.96 | custom fusion | flops 1179648 | bytes 590336 | tf_op jit(solution)/shard_map/transpose(jvp())/scatter-add | solution.py:68
  144.6 9.3 %gather_fusion.5 = f32[2048,576]{1,0:T(8,128)} fusion(f32[256,576]{1,0:T(8,128)S(1)} %broadcast_multiply_fusion.2, s32[2048]{0:T(1024)S(1)} %copy-done.22), kind=kCustom, calls=%fused_computation.5 | custom fusion | bytes 9445376 | tf_op jit(solution)/shard_map/transpose(jvp())/gather | solution.py:67
  153.9 5.8 %copy.46 = f32[2048,576]{0,1:T(8,128)} copy(f32[2048,576]{1,0:T(8,128)} %gather_fusion.5) | data formatting | bytes 9437184 | tf_op jit(solution)/shard_map/transpose(jvp())/gather | solution.py:67
  159.7 3.5 %multiply_reduce_fusion = (f32[2048,64]{0,1:T(8,128)S(1)}, f32[2048,9]{0,1:T(8,128)S(1)}) fusion(f32[2048,9,64]{0,2,1:T(8,128)} %bitcast.70, f32[2048,9]{0,1:T(8,128)S(1)} %bitcast.75, pred[2048]{0:T(1024)(128)(4,1)S(1)} %get-tuple-element.13, f32[2048,64]{0,1:T(8,128)S(1)} %convolution_multiply_fusion), kind=kLoop, calls=%fused_computation.12 | loop fusion | flops 5748736 | bytes 5916672 | tf_op jit(solution)/shard_map/transpose(jvp())/reduce_sum | solution.py:66
  166.9 2.1 fusion.57
  169.6 11.8 %scatter_custom_fusion.4 = f32[1280,3]{1,0:T(8,128)S(1)} fusion(s32[2048]{0:T(1024)} %param.18, f32[2048,3]{1,0:T(8,128)S(1)} %copy.47, f32[]{:T(128)} %constant.24.clone.1), kind=kCustom, calls=%fused_computation.92 | custom fusion | flops 6144 | bytes 15872 | tf_op jit(solution)/shard_map/scatter-add | solution.py:125
  181.8 5.1 %collective-permute-start.5 = (f32[1,3,3,128]{3,2,1,0:T(4,128)S(1)}, f32[1,3,3,128]{3,2,1,0:T(4,128)S(1)}, u32[]{:S(2)}, u32[]{:S(2)}) collective-permute-start(f32[1,3,3,128]{3,2,1,0:T(4,128)S(1)} %get-tuple-element.39), channel_id=1, source_target_pairs={{8,0},{16,8},{24,16},{32,24},{40,32},{48,40},{56,48},{64,56},{72,6... | collective-permute-start | bytes 13832 | tf_op jit(solution)/shard_map/ppermute | solution.py:18
  187.9 2.6 %collective-permute-start.6 = (f32[5,1,3,128]{3,2,1,0:T(4,128)S(1)}, f32[5,1,3,128]{3,2,1,0:T(4,128)S(1)}, u32[]{:S(2)}, u32[]{:S(2)}) collective-permute-start(f32[5,1,3,128]{3,2,1,0:T(4,128)S(1)} %get-tuple-element.36), channel_id=1, source_target_pairs={{0,1},{1,2},{2,3},{3,4},{4,5},{5,6},{6,7},{7,0},{8,9},{9,10},{10,1... | collective-permute-start | bytes 23048 | tf_op jit(solution)/shard_map/ppermute | solution.py:16
  192.6 11.6 %scatter_custom_fusion.3 = f32[256,3]{1,0:T(8,128)S(1)} fusion(s32[2048]{0:T(1024)} %param.17, f32[2048,3]{1,0:T(8,128)S(1)} %copy.47, f32[]{:T(128)} %constant.24.clone.1), kind=kCustom, calls=%fused_computation.117 | custom fusion | flops 6144 | bytes 3584 | tf_op jit(solution)/shard_map/scatter-add | solution.py:124
  204.2 15.4 %scatter_custom_fusion.1 = f32[256]{0:T(256)} fusion(s32[2048]{0:T(1024)} %param.17, f32[2048]{0:T(1024)S(1)} %get-tuple-element.49, f32[]{:T(128)} %constant.24.clone.1), kind=kCustom, calls=%fused_computation.196 | custom fusion | flops 2048 | bytes 1536 | tf_op jit(solution)/shard_map/jvp()/scatter-add | solution.py:83
  (158 shorter events, 36.1 us)
Async XLA Ops:
  0.6 114.3 %copy-start = (bf16[256,256]{1,0:T(8,128)(2,1)S(1)}, bf16[256,256]{1,0:T(8,128)(2,1)}, u32[]{:S(2)}) copy-start(bf16[256,256]{1,0:T(8,128)(2,1)} %param.28) | copy-start | bytes 393220
  3.0 45.6 %collective-permute-start.1 = (bf16[1,1,128,256]{3,2,1,0:T(8,128)(2,1)S(1)}, bf16[1,1,128,256]{3,2,1,0:T(8,128)(2,1)S(1)}, u32[]{:S(2)}, u32[]{:S(2)}) collective-permute-start(bf16[1,1,128,256]{3,2,1,0:T(8,128)(2,1)S(1)} %bitcast.80), channel_id=1, source_target_pairs={{8,0},{16,8},{24,16},{32,24},{40,32},{48,40},{56,48},{64,56},{72,6... | collective-permute-start | bytes 196616 | tf_op jit(solution)/shard_map/ppermute | solution.py:18
  10.1 38.5 %collective-permute-start = (bf16[1,1,128,256]{3,2,1,0:T(8,128)(2,1)S(1)}, bf16[1,1,128,256]{3,2,1,0:T(8,128)(2,1)S(1)}, u32[]{:S(2)}, u32[]{:S(2)}) collective-permute-start(bf16[1,1,128,256]{3,2,1,0:T(8,128)(2,1)S(1)} %bitcast.81), channel_id=1, source_target_pairs={{0,8},{8,16},{16,24},{24,32},{32,40},{40,48},{48,56},{56,64},{64,7... | collective-permute-start | bytes 196616 | tf_op jit(solution)/shard_map/ppermute | solution.py:16
  11.6 10.6 %copy-start.16 = (f32[2048]{0:T(1024)}, f32[2048]{0:T(1024)S(1)}, u32[]{:S(2)}) copy-start(f32[2048]{0:T(1024)S(1)} %multiply_reduce_fusion.5) | copy-start | bytes 24580
  12.9 11.8 %copy-start.21 = (s32[2048]{0:T(1024)}, s32[2048]{0:T(1024)S(1)}, u32[]{:S(2)}) copy-start(s32[2048]{0:T(1024)S(1)} %get-tuple-element.48) | copy-start | bytes 24580
  13.6 8.7 %copy-start.18 = (f32[2048]{0:T(1024)}, f32[2048]{0:T(1024)S(1)}, u32[]{:S(2)}) copy-start(f32[2048]{0:T(1024)S(1)} %get-tuple-element.45) | copy-start | bytes 24580
  24.7 26.1 %copy-start.31 = (s32[2048]{0:T(1024)S(1)}, s32[2048]{0:T(1024)}, u32[]{:S(2)}) copy-start(s32[2048]{0:T(1024)} %param.18) | copy-start | bytes 24580
  46.8 7.5 %copy-start.2 = (bf16[256,256]{1,0:T(8,128)(2,1)S(1)}, bf16[256,256]{1,0:T(8,128)(2,1)}, u32[]{:S(2)}) copy-start(bf16[256,256]{1,0:T(8,128)(2,1)} %param.16) | copy-start | bytes 393220
  46.8 7.5 %copy-start.10 = (bf16[256,256]{1,0:T(8,128)(2,1)S(1)}, bf16[256,256]{1,0:T(8,128)(2,1)}, u32[]{:S(2)}) copy-start(bf16[256,256]{1,0:T(8,128)(2,1)} %param.23) | copy-start | bytes 393220
  48.7 5.4 %collective-permute-start.3 = (bf16[3,1,128,256]{3,2,1,0:T(8,128)(2,1)S(1)}, bf16[3,1,128,256]{3,2,1,0:T(8,128)(2,1)S(1)}, u32[]{:S(2)}, u32[]{:S(2)}) collective-permute-start(bf16[3,1,128,256]{3,2,1,0:T(8,128)(2,1)S(1)} %pad_maximum_fusion.2), channel_id=1, source_target_pairs={{1,0},{2,1},{3,2},{4,3},{5,4},{6,5},{7,6},{0,7},{9,8},{10,9},{11,1... | collective-permute-start | bytes 589832 | tf_op jit(solution)/shard_map/ppermute | solution.py:18
  49.7 4.5 %collective-permute-start.2 = (bf16[3,1,128,256]{3,2,1,0:T(8,128)(2,1)S(1)}, bf16[3,1,128,256]{3,2,1,0:T(8,128)(2,1)S(1)}, u32[]{:S(2)}, u32[]{:S(2)}) collective-permute-start(bf16[3,1,128,256]{3,2,1,0:T(8,128)(2,1)S(1)} %pad_maximum_fusion.2), channel_id=1, source_target_pairs={{0,1},{1,2},{2,3},{3,4},{4,5},{5,6},{6,7},{7,0},{8,9},{9,10},{10,1... | collective-permute-start | bytes 589832 | tf_op jit(solution)/shard_map/ppermute | solution.py:16
  64.2 6.1 %copy-start.13 = (bf16[256,64]{0,1:T(8,128)(2,1)S(1)}, bf16[256,64]{0,1:T(8,128)(2,1)}, u32[]{:S(2)}) copy-start(bf16[256,64]{0,1:T(8,128)(2,1)} %param.24) | copy-start | bytes 98308
  64.2 6.4 %copy-start.3 = (f32[9,2048]{1,0:T(8,128)S(1)}, f32[9,2048]{1,0:T(8,128)}, u32[]{:S(2)}) copy-start(f32[9,2048]{1,0:T(8,128)} %stack.2) | copy-start | bytes 221188
  73.4 5.8 %copy-start.25 = (s32[2048]{0:T(1024)S(1)}, s32[2048]{0:T(1024)}, u32[]{:S(2)}) copy-start(s32[2048]{0:T(1024)} %param.17) | copy-start | bytes 24580
  123.9 20.6 %copy-start.22 = (s32[2048]{0:T(1024)S(1)}, s32[2048]{0:T(1024)}, u32[]{:S(2)}) copy-start(s32[2048]{0:T(1024)} %copy-done.21) | copy-start | bytes 24580
  159.7 4.2 %copy-start.12 = (bf16[256,256]{1,0:T(8,128)(2,1)S(1)}, bf16[256,256]{1,0:T(8,128)(2,1)}, u32[]{:S(2)}) copy-start(bf16[256,256]{1,0:T(8,128)(2,1)} %param.26) | copy-start | bytes 393220
  159.7 4.2 %copy-start.38 = (f32[2048,256]{0,1:T(8,128)S(1)}, f32[2048,256]{0,1:T(8,128)}, u32[]{:S(2)}) copy-start(f32[2048,256]{0,1:T(8,128)} %get-tuple-element.51) | copy-start | bytes 6291460
  159.7 4.2 %copy-start.40 = (bf16[2048,256]{0,1:T(8,128)(2,1)S(1)}, bf16[2048,256]{0,1:T(8,128)(2,1)}, u32[]{:S(2)}) copy-start(bf16[2048,256]{0,1:T(8,128)(2,1)} %copy-done.39) | copy-start | bytes 3145732
  169.0 12.6 %copy-start.32 = (f32[9]{0:T(128)S(1)}, f32[9]{0:T(128)}, u32[]{:S(2)}) copy-start(f32[9]{0:T(128)} %pad.28.clone) | copy-start | bytes 112
  169.2 52.4 %copy-start.1 = (bf16[256,256]{1,0:T(8,128)(2,1)S(1)}, bf16[256,256]{1,0:T(8,128)(2,1)}, u32[]{:S(2)}) copy-start(bf16[256,256]{1,0:T(8,128)(2,1)} %param.28) | copy-start | bytes 393220
  181.7 6.2 %collective-permute-start.4 = (f32[1,3,3,128]{3,2,1,0:T(4,128)S(1)}, f32[1,3,3,128]{3,2,1,0:T(4,128)S(1)}, u32[]{:S(2)}, u32[]{:S(2)}) collective-permute-start(f32[1,3,3,128]{3,2,1,0:T(4,128)S(1)} %get-tuple-element.38), channel_id=1, source_target_pairs={{0,8},{8,16},{16,24},{24,32},{32,40},{40,48},{48,56},{56,64},{64,7... | collective-permute-start | bytes 13832 | tf_op jit(solution)/shard_map/ppermute | solution.py:16
  181.8 6.1 %collective-permute-start.5 = (f32[1,3,3,128]{3,2,1,0:T(4,128)S(1)}, f32[1,3,3,128]{3,2,1,0:T(4,128)S(1)}, u32[]{:S(2)}, u32[]{:S(2)}) collective-permute-start(f32[1,3,3,128]{3,2,1,0:T(4,128)S(1)} %get-tuple-element.39), channel_id=1, source_target_pairs={{8,0},{16,8},{24,16},{32,24},{40,32},{48,40},{56,48},{64,56},{72,6... | collective-permute-start | bytes 13832 | tf_op jit(solution)/shard_map/ppermute | solution.py:18
  187.9 31.7 %collective-permute-start.6 = (f32[5,1,3,128]{3,2,1,0:T(4,128)S(1)}, f32[5,1,3,128]{3,2,1,0:T(4,128)S(1)}, u32[]{:S(2)}, u32[]{:S(2)}) collective-permute-start(f32[5,1,3,128]{3,2,1,0:T(4,128)S(1)} %get-tuple-element.36), channel_id=1, source_target_pairs={{0,1},{1,2},{2,3},{3,4},{4,5},{5,6},{6,7},{7,0},{8,9},{9,10},{10,1... | collective-permute-start | bytes 23048 | tf_op jit(solution)/shard_map/ppermute | solution.py:16
  190.5 29.0 %collective-permute-start.7 = (f32[5,1,3,128]{3,2,1,0:T(4,128)S(1)}, f32[5,1,3,128]{3,2,1,0:T(4,128)S(1)}, u32[]{:S(2)}, u32[]{:S(2)}) collective-permute-start(f32[5,1,3,128]{3,2,1,0:T(4,128)S(1)} %get-tuple-element.37), channel_id=1, source_target_pairs={{1,0},{2,1},{3,2},{4,3},{5,4},{6,5},{7,6},{0,7},{9,8},{10,9},{11,1... | collective-permute-start | bytes 23048 | tf_op jit(solution)/shard_map/ppermute | solution.py:18
  (27 other events, 49.7 us)
where the time goes:
time: 224 us; the launch traced here: 222 us
  local copies, waits for them, and re-layouts  91.4 us (41%)
  other arithmetic  88.3 us (39%)
  starting transfers between devices  19.1 us (9%)
  matrix products  17.7 us (8%)
  waiting for transfers between devices  3.68 us (2%)
    gather x1, local copies, waits for them, and re-layouts, edge_energies(): return jax.ops.segment_sum(energy, centre, num_segments=atoms)  22 us
    gather x4, local copies, waits for them, and re-layouts, per_device(): pre = centre_proj[centre] + table_proj[nbr_slot]  18 us
    scatter-add x1, other arithmetic, edge_energies(): return jax.ops.segment_sum(energy, centre, num_segments=atoms)  15.4 us
    ppermute x4, starting transfers between devices, padded_2(): lax.ppermute(head, axis, [((i + 1) % count, i) for i in range(count)])  15.2 us
    gather x2, local copies, waits for them, and re-layouts, edge_energies(): env = jax.ops.segment_sum(spread, centre, num_segments=atoms) * 0.125  15.1 us
    gather x2, local copies, waits for them, and re-layouts, edge_energies(): local = env[centre].reshape(count, 9, chan) * harm.T[:, :, None]  15.1 us
    scatter-add x1, other arithmetic, edge_energies(): local = env[centre].reshape(count, 9, chan) * harm.T[:, :, None]  14.8 us
    scatter-add x1, other arithmetic, edge_energies(): env = jax.ops.segment_sum(spread, centre, num_segments=atoms) * 0.125  14.7 us
  transfers between devices with their start and end apart: 8, of which 2 were waited for; matrix products, arithmetic and copies ran while one was open for 30% of the time, Pallas kernels for 0%

commit v1 on v0

v1 whole, which is shorter than its diff:
```python
import functools
import math

import jax
import jax.numpy as jnp
from jax import lax
from jax.experimental import pallas as pl
from jax.experimental.pallas import tpu as pltpu
from jax.sharding import PartitionSpec as P

F32 = jnp.float32
BF16 = jnp.bfloat16
MESH = pl.DeviceIdType.MESH
OFFSETS = ((-1, -1), (-1, 0), (-1, 1), (0, -1), (0, 1), (1, -1), (1, 0), (1, 1))
CUTOFF = 5.0
R3, R5, R15 = math.sqrt(3.0), math.sqrt(5.0), math.sqrt(15.0)
DEGREES = ((0,), (1, 2, 3), (4, 5, 6, 7, 8))
WIDTH = 256
C = 64


def mm(lhs, rhs):
    return jnp.dot(lhs, rhs, preferred_element_type=F32)


def mm_nt(lhs, rhs):
    return lax.dot_general(lhs, rhs, (((1,), (1,)), ((), ())), preferred_element_type=F32)


def turned(block):
    return block.astype(F32).T.astype(BF16)


def neighbours(space, grp):
    me_s, me_g = lax.axis_index("space"), lax.axis_index("grp")
    return [(lax.rem(me_s + a + space, space), lax.rem(me_g + b + grp, grp)) for a, b in OFFSETS]


def onehot(row, count, first=0):
    ids = lax.broadcasted_iota(jnp.int32, (count, row.shape[1]), 0) + first
    return jnp.where(ids == row, 1.0, 0.0).astype(BF16)


def greet(peers):
    barrier = pltpu.get_barrier_semaphore()
    for peer in peers:
        pl.semaphore_signal(barrier, inc=1, device_id=peer, device_id_type=MESH)
    return barrier


def exchange(peers, source, landing, send_sem, recv_sem):
    return [
        pltpu.make_async_remote_copy(
            src_ref=source(c),
            dst_ref=landing.at[7 - c],
            send_sem=send_sem.at[c],
            recv_sem=recv_sem.at[7 - c],
            device_id=peer,
            device_id_type=MESH,
        )
        for c, peer in enumerate(peers)
    ]


def geometry(vec_ref, centre_ref, slot_ref, geo_ref, dense):
    for i in range(3):
        for b in range(16):
            dense[i, b : b + 1, :] = vec_ref[i : i + 1, b * 128 : (b + 1) * 128]
    vx, vy, vz = dense[0], dense[1], dense[2]
    dist = jnp.sqrt(vx * vx + vy * vy + vz * vz)
    inv = 1.0 / dist
    t = dist / CUTOFF
    angle = math.pi * t
    sin1, cos1 = jnp.sin(angle), jnp.cos(angle)
    scale = math.sqrt(2.0 / CUTOFF)
    sins, coss = [jnp.zeros_like(t), sin1], [jnp.ones_like(t), cos1]
    for n in range(2, 9):
        sins.append(2.0 * cos1 * sins[-1] - sins[-2])
        coss.append(2.0 * cos1 * coss[-1] - coss[-2])
    for n in range(1, 9):
        radial = scale * sins[n] * inv
        geo_ref[0, :, n - 1, :] = radial
        geo_ref[1, :, n - 1, :] = (scale * n * math.pi / CUTOFF * coss[n] - radial) * inv
    t2 = t * t
    t4 = t2 * t2
    t5, t6, t7, t8 = t4 * t, t4 * t2, t4 * t2 * t, t4 * t4
    geo_ref[2, :, 0, :] = vx * inv
    geo_ref[2, :, 1, :] = vy * inv
    geo_ref[2, :, 2, :] = vz * inv
    geo_ref[2, :, 3, :] = inv
    geo_ref[2, :, 4, :] = 1.0 - 28.0 * t6 + 48.0 * t7 - 21.0 * t8
    geo_ref[2, :, 5, :] = (336.0 * t6 - 168.0 * t5 - 168.0 * t7) / CUTOFF
    geo_ref[2, :, 6, :] = centre_ref[...].astype(F32)
    geo_ref[2, :, 7, :] = slot_ref[...].astype(F32)


def first_kernel(
    space, grp,
    vec_ref, feat_ref, centre_ref, slot_ref, rows_ref, w_radial_ref, w_centre_ref, w_nbr_ref, w_env_ref, w_val_ref,
    w_mix_ref, w_scal_ref, w_read_ref, w_out_ref,
    tab_ref, own_ref, cen_ref, geo_ref, wr_ref, wrhl_ref, wev_ref, wevt_ref, wmixt_ref, wscalt_ref, wreadt_ref, wout_ref,
    outgoing, dense, send_sem, recv_sem,
):
    peers = neighbours(space, grp)
    barrier = greet(peers)
    own = mm(feat_ref[...], w_nbr_ref[...]).T.astype(BF16)
    own_ref[...] = own
    outgoing[...] = mm(own, onehot(rows_ref[...], WIDTH)).astype(BF16)
    pl.semaphore_wait(barrier, 8)
    copies = exchange(peers, lambda c: outgoing, tab_ref, send_sem, recv_sem)
    for copy in copies:
        copy.start()
    cen_ref[...] = mm(feat_ref[...], w_centre_ref[...]).T.astype(BF16)
    geometry(vec_ref, centre_ref, slot_ref, geo_ref, dense)
    w_radial = w_radial_ref[...]
    high = w_radial.astype(BF16).astype(F32)
    low = w_radial - high
    stacked = jnp.concatenate([high, low, high, jnp.zeros((104, WIDTH), F32)], axis=0)
    wr_ref[...] = stacked.T[:, :32].astype(BF16)
    wrhl_ref[...] = jnp.concatenate([high, low], axis=0).astype(BF16)
    both = jnp.concatenate([w_env_ref[...].astype(F32), w_val_ref[...].astype(F32)], axis=1)
    wev_ref[...] = both.astype(BF16)
    wevt_ref[...] = both.T.astype(BF16)
    wmixt_ref[...] = turned(w_mix_ref[...])
    scal = jnp.concatenate([w_scal_ref[...].astype(F32), jnp.zeros((64, WIDTH), F32)], axis=0)
    wscalt_ref[...] = scal.T[:, :192].astype(BF16)
    wreadt_ref[...] = turned(w_read_ref[...])
    wout_ref[...] = jnp.broadcast_to(w_out_ref[...], (128, WIDTH)).T
    for copy in copies:
        copy.wait_send()
        copy.wait_recv()


def harmonics(x, y, z):
    return [
        None, R3 * x, R3 * y, R3 * z,
        R15 * x * y, R15 * y * z, 0.5 * R5 * (3.0 * z * z - 1.0), R15 * x * z, 0.5 * R15 * (x * x - y * y),
    ]


def scaled(block, harm):
    return block if harm is None else block * harm


def part(block, i):
    return block[i * C : (i + 1) * C]


def down(block):
    return jnp.sum(block, axis=0, keepdims=True)


def compact(mask_ref, geo_ref, packed):
    packed[0] = jnp.zeros_like(packed[0])
    packed[1] = jnp.zeros_like(packed[1])
    sub = lax.broadcasted_iota(jnp.int32, packed.shape[1:], 1)
    packed[2] = jnp.where(sub >= 6, -1.0, 0.0)
    lane = lax.broadcasted_iota(jnp.int32, (8, 128), 1)
    start = jnp.int32(0)
    for b in range(16):
        count = jnp.sum(mask_ref[b : b + 1, :].astype(F32)).astype(jnp.int32)
        row, shift = lax.shift_right_logical(start, 7), lax.bitwise_and(start, 127)
        here = (lane >= shift) & (lane < shift + count)
        spill = lane < shift + count - 128
        for g in range(3):
            moved = pltpu.roll(geo_ref[g, b], shift, 1)
            packed[g, row] = jnp.where(here, moved, packed[g, row])
            packed[g, row + 1] = jnp.where(spill, moved, packed[g, row + 1])
        start = start + count
    return start


def main_kernel(
    span,
    mask_ref, geo_ref, tab_ref, own_ref, cen_ref, wr_ref, wrhl_ref, wev_ref, wevt_ref, wmixt_ref, wscalt_ref, wreadt_ref,
    wout_ref, w_mix_ref, w_scal_ref, w_read_ref,
    energy_ref, force_ref, sums_ref,
    packed, lat_s, act_s, slope_s, wv_s, back_s, vbar_s, hbar_s, en_s, env_s, envbar_s, envh_s, fsum, csum,
):
    wide = span // 128
    total = compact(mask_ref, geo_ref, packed)
    chunks = lax.div(total + (span - 1), span)
    env_s[...] = jnp.zeros_like(env_s)
    envbar_s[...] = jnp.zeros_like(envbar_s)
    fsum[...] = jnp.zeros_like(fsum)
    csum[...] = jnp.zeros_like(csum)

    def rows(group, j):
        return jnp.concatenate([packed[group, wide * j + i] for i in range(wide)], axis=1)

    def fields(j):
        geo = rows(2, j)
        return [geo[i : i + 1] for i in range(8)]

    def forward(j, carry):
        x, y, z, _, envelope, _, centre, slot = fields(j)
        centre, slot = centre.astype(jnp.int32), slot.astype(jnp.int32)
        radial = rows(0, j)
        high = radial.astype(BF16).astype(F32)
        stacked = jnp.concatenate([high, high, radial - high, jnp.zeros_like(high)], axis=0).astype(BF16)
        hot = onehot(centre, WIDTH)
        lifted = mm(wr_ref[...], stacked) + mm(cen_ref[...], hot) + mm(own_ref[...], onehot(slot, WIDTH))
        for pair in range(4):
            block = jnp.concatenate([tab_ref[2 * pair], tab_ref[2 * pair + 1]], axis=1)
            lifted = lifted + mm(block, onehot(slot, WIDTH, WIDTH * (pair + 1)))
        gate = 1.0 / (1.0 + jnp.exp(-lifted))
        active = lifted * gate
        act_s[j] = active
        slope_s[j] = gate + active * (1.0 - gate)
        latent = (active * envelope).astype(BF16)
        lat_s[j] = latent
        wv = mm(wevt_ref[...], latent)
        wv_s[j] = wv
        weights = wv[:C]
        harm = harmonics(x, y, z)
        spread = jnp.concatenate([scaled(weights, harm[i]).astype(BF16) for i in range(9)], axis=0)
        env_s[...] += mm_nt(spread, hot)
        return carry

    lax.fori_loop(0, chunks, forward, 0)
    envh_s[...] = (env_s[...] * 0.125).astype(BF16)

    def middle(j, carry):
        x, y, z, _, _, _, centre, _ = fields(j)
        hot = onehot(centre.astype(jnp.int32), WIDTH)
        harm = harmonics(x, y, z)
        local = mm(envh_s[...], hot)
        values = wv_s[j, C:]
        invariants = []
        for degree in DEGREES:
            whole = None
            for i in degree:
                term = scaled(part(local, i), harm[i])
                whole = term if whole is None else whole + term
            invariants.append(whole)
        scal = jnp.concatenate([(q * values).astype(BF16) for q in invariants], axis=0)
        latent = lat_s[j]
        update = mm(wmixt_ref[...], latent) + mm(wscalt_ref[...], scal)
        gate = 1.0 / (1.0 + jnp.exp(-update))
        active = update * gate
        slope = gate + active * (1.0 - gate)
        mixed = (latent.astype(F32) + active).astype(BF16)
        hidden = mm(wreadt_ref[...], mixed)
        gate_h = 1.0 / (1.0 + jnp.exp(-hidden))
        active_h = hidden * gate_h
        out = jnp.concatenate([wout_ref[...]] * wide, axis=1)
        en_s[j] = down(active_h * out)
        hidden_bar = (out * (gate_h + active_h * (1.0 - gate_h))).astype(BF16)
        mixed_bar = mm(w_read_ref[...], hidden_bar).astype(BF16).astype(F32)
        update_bar = (mixed_bar * slope).astype(BF16)
        back_s[j] = mixed_bar + mm(w_mix_ref[...], update_bar)
        scal_bar = mm(w_scal_ref[...], update_bar)
        values_bar = None
        locals_bar, harm_bar = [], []
        for level, degree in enumerate(DEGREES):
            bar = part(scal_bar, level)
            term = bar * invariants[level]
            values_bar = term if values_bar is None else values_bar + term
            inner = bar * values
            for i in degree:
                locals_bar.append(scaled(inner, harm[i]).astype(BF16))
                if i:
                    harm_bar.append(down(part(local, i) * inner))
        vbar_s[j] = values_bar.astype(BF16)
        hbar_s[j] = jnp.concatenate(harm_bar, axis=0)
        envbar_s[...] += mm_nt(jnp.concatenate(locals_bar, axis=0), hot)
        return carry

    lax.fori_loop(0, chunks, middle, 0)
    envh_s[...] = (envbar_s[...] * 0.125).astype(BF16)

    def backward(j, carry):
        x, y, z, inv, envelope, slope_env, centre, slot = fields(j)
        slot = slot.astype(jnp.int32)
        hot = onehot(centre.astype(jnp.int32), WIDTH)
        harm = harmonics(x, y, z)
        spread_bar = mm(envh_s[...], hot)
        weights = wv_s[j, :C]
        weights_bar = part(spread_bar, 0)
        for i in range(1, 9):
            weights_bar = weights_bar + part(spread_bar, i) * harm[i]
        harm_bar = hbar_s[j]
        bars = [None] + [harm_bar[i - 1 : i] + down(part(spread_bar, i) * weights) for i in range(1, 9)]
        wv_bar = jnp.concatenate([weights_bar.astype(BF16), vbar_s[j]], axis=0)
        latent_bar = back_s[j] + mm(wev_ref[...], wv_bar)
        envelope_bar = down(latent_bar * act_s[j])
        lifted_bar = (latent_bar * envelope * slope_s[j]).astype(BF16)
        radial_bar = mm(wrhl_ref[...], lifted_bar)
        dist_bar = down((radial_bar[:8] + radial_bar[8:]) * rows(1, j)) + envelope_bar * slope_env
        ux = R3 * bars[1] + R15 * (y * bars[4] + z * bars[7] + x * bars[8])
        uy = R3 * bars[2] + R15 * (x * bars[4] + z * bars[5] - y * bars[8])
        uz = R3 * bars[3] + R15 * (y * bars[5] + x * bars[7]) + 3.0 * R5 * z * bars[6]
        along = dist_bar - (x * ux + y * uy + z * uz) * inv
        grads = jnp.concatenate([ux * inv + x * along, uy * inv + y * along, uz * inv + z * along, en_s[j]], axis=0)
        top = grads.astype(BF16).astype(F32)
        both = jnp.concatenate([top, grads - top], axis=0)
        csum[...] += mm_nt(both.astype(BF16), hot)
        block = lax.shift_right_arithmetic(slot, 7)
        lo = onehot(lax.bitwise_and(slot, 127), 128)
        split = jnp.concatenate([jnp.where(block == h, both, 0.0) for h in range(10)], axis=0).astype(BF16)
        fsum[...] += mm_nt(split, lo)
        return carry

    lax.fori_loop(0, chunks, backward, 0)
    centre_sum = csum[0:4] + csum[4:8]
    energy_ref[...] = centre_sum[3:4]
    own = jnp.concatenate([fsum[0:4] + fsum[4:8], fsum[8:12] + fsum[12:16]], axis=1)
    force_ref[...] = (centre_sum - own)[0:3]
    for c in range(8):
        first = 16 + 8 * c
        sums_ref[c, 0:4] = fsum[first : first + 4] + fsum[first + 4 : first + 8]
        sums_ref[c, 4:8] = jnp.zeros((4, 128), F32)


def last_kernel(space, grp, sums_ref, force_ref, rows_ref, out_ref, landed, send_sem, recv_sem):
    peers = neighbours(space, grp)
    barrier = greet(peers)
    pl.semaphore_wait(barrier, 8)
    copies = exchange(peers, lambda c: sums_ref.at[c], landed, send_sem, recv_sem)
    for copy in copies:
        copy.start()
    hot = onehot(rows_ref[...], WIDTH)
    for copy in copies:
        copy.wait_send()
        copy.wait_recv()
    total = landed[0]
    for c in range(1, 8):
        total = total + landed[c]
    top = total.astype(BF16).astype(F32)
    both = jnp.concatenate([top, total - top], axis=0).astype(BF16)
    away = mm_nt(both, hot)
    out_ref[...] = force_ref[...] - (away[0:3] + away[8:11])


def per_device(
    space, grp,
    rel_vec, atom_feat, centre, nbr_slot, edge_mask, send_rows, w_radial, w_centre, w_nbr, w_env, w_val, w_mix, w_scal,
    w_read, w_out,
):
    span = 256
    chunks = 2048 // span
    vmem = pl.BlockSpec(memory_space=pltpu.VMEM)
    shape = jax.ShapeDtypeStruct
    limit = 56 * 1024 * 1024
    tab, own, cen, geo, wr, wrhl, wev, wevt, wmixt, wscalt, wreadt, wout = pl.pallas_call(
        functools.partial(first_kernel, space, grp),
        out_shape=[
            shape((8, WIDTH, 128), BF16), shape((WIDTH, WIDTH), BF16), shape((WIDTH, WIDTH), BF16), shape((3, 16, 8, 128), F32),
            shape((WIDTH, 32), BF16), shape((16, WIDTH), BF16), shape((WIDTH, 128), BF16), shape((128, WIDTH), BF16),
            shape((WIDTH, WIDTH), BF16), shape((WIDTH, 192), BF16), shape((WIDTH, WIDTH), BF16), shape((WIDTH, 128), F32),
        ],
        in_specs=[vmem] * 14,
        out_specs=[vmem] * 12,
        scratch_shapes=[
            pltpu.VMEM((WIDTH, 128), BF16),
            pltpu.VMEM((3, 16, 128), F32),
            pltpu.SemaphoreType.DMA((8,)),
            pltpu.SemaphoreType.DMA((8,)),
        ],
        compiler_params=pltpu.CompilerParams(collective_id=0, has_side_effects=True, vmem_limit_bytes=limit),
        name="exchange_rows",
    )(
        rel_vec, atom_feat, centre.reshape(16, 128), nbr_slot.reshape(16, 128), send_rows, w_radial, w_centre, w_nbr, w_env,
        w_val, w_mix, w_scal, w_read, w_out.reshape(1, WIDTH),
    )
    energy, force, sums = pl.pallas_call(
        functools.partial(main_kernel, span),
        out_shape=[shape((1, WIDTH), F32), shape((3, WIDTH), F32), shape((8, 8, 128), F32)],
        in_specs=[vmem] * 16,
        out_specs=[vmem] * 3,
        scratch_shapes=[
            pltpu.VMEM((3, 18, 8, 128), F32),
            pltpu.VMEM((chunks, WIDTH, span), BF16),
            pltpu.VMEM((chunks, WIDTH, span), F32),
            pltpu.VMEM((chunks, WIDTH, span), F32),
            pltpu.VMEM((chunks, 2 * C, span), F32),
            pltpu.VMEM((chunks, WIDTH, span), F32),
            pltpu.VMEM((chunks, C, span), BF16),
            pltpu.VMEM((chunks, 8, span), F32),
            pltpu.VMEM((chunks, 1, span), F32),
            pltpu.VMEM((9 * C, WIDTH), F32),
            pltpu.VMEM((9 * C, WIDTH), F32),
            pltpu.VMEM((9 * C, WIDTH), BF16),
            pltpu.VMEM((80, 128), F32),
            pltpu.VMEM((8, WIDTH), F32),
        ],
        compiler_params=pltpu.CompilerParams(vmem_limit_bytes=limit),
        name="edges",
    )(edge_mask.reshape(16, 128), geo, tab, own, cen, wr, wrhl, wev, wevt, wmixt, wscalt, wreadt, wout, w_mix, w_scal, w_read)
    forces = pl.pallas_call(
        functools.partial(last_kernel, space, grp),
        out_shape=shape((3, WIDTH), F32),
        in_specs=[vmem] * 3,
        out_specs=vmem,
        scratch_shapes=[
            pltpu.VMEM((8, 8, 128), F32),
            pltpu.SemaphoreType.DMA((8,)),
            pltpu.SemaphoreType.DMA((8,)),
        ],
        compiler_params=pltpu.CompilerParams(collective_id=1, has_side_effects=True, vmem_limit_bytes=limit),
        name="return_sums",
    )(sums, force, send_rows)
    return (energy.reshape(WIDTH), forces)


def solution(mesh):
    edges = P(("space", "grp"))
    placed = (
        P(None, ("space", "grp")), P(("space", "grp"), None), edges, edges, edges, P(("space", "grp"), None),
    ) + (P(),) * 9
    return jax.shard_map(
        functools.partial(per_device, mesh.shape["space"], mesh.shape["grp"]),
        mesh=mesh,
        in_specs=placed,
        out_specs=(edges, P(None, ("space", "grp"))),
        check_vma=False,
    )
```

time: 224 us -> 48.9 us (0.22)
  other arithmetic: 88.3 us -> 0 us
  local copies, waits for them, and re-layouts: 91.4 us -> 3.5 us
  Pallas kernels: 0 us -> 44.4 us
  starting transfers between devices: 19.1 us -> 0 us
  matrix products: 17.7 us -> 0 us
  waiting for transfers between devices: 3.68 us -> 0 us
    gather x10 -> x0, local copies, waits for them, and re-layouts: 72 us -> none  [the longest x1 22 us: edge_energies(): return jax.ops.segment_sum(energy, centre, num_segments=atoms)]
    scatter-add x6 -> x0, other arithmetic: 69.4 us -> none  [the longest x1 15.4 us: edge_energies(): return jax.ops.segment_sum(energy, centre, num_segments=atoms)]
    pallas_call x0 -> x3, Pallas kernels: none -> 44.4 us  [the longest x1 16.6 us: per_device(): pl.pallas_call(functools.partial(first_kernel, space, grp), out_shape=[sh...]
    ppermute x8 -> x0, starting transfers between devices: 19.1 us -> none  [the longest x4 15.2 us: padded_2(): lax.ppermute(head, axis, [((i + 1) % count, i) for i in range(count)])]
    dot_general x14 -> x0, matrix products: 17.7 us -> none  [the longest x2 8.22 us: edge_energies(): lifted = jnp.dot(radial.T, w_radial, precision=lax.Precision.HIGHEST) + pre]
    mul x10 -> x0, other arithmetic: 9.21 us -> none  [the longest x2 5.58 us: edge_energies(): local = env[centre].reshape(count, 9, chan) * harm.T[:, :, None]]
    reshape x1 -> x0, local copies, waits for them, and re-layouts: 5.78 us -> none  [edge_energies(): local = env[centre].reshape(count, 9, chan) * harm.T[:, :, None]]
    mul x1 -> x0, local copies, waits for them, and re-layouts: 5.78 us -> none  [edge_energies(): spread = (harm.T[:, :, None] * weights[:, None, :]).reshape(count, 9 * chan)]
  transfers between devices with their start and end apart: 8 -> 0, of which waited for: 2 -> 0; matrix products, arithmetic and copies ran while one was open for 30% -> 0% of each run, Pallas kernels for 0% -> 0%
where the time goes in v1:
time: 48.9 us; the launch traced here: 48.5 us
  Pallas kernels  44.4 us (91%)
  local copies, waits for them, and re-layouts  3.5 us (7%)
  between operations  0.66 us (1%)
    pallas_call x1, Pallas kernels, per_device(): pl.pallas_call(functools.partial(first_kernel, space, grp), out_shape=[sh...  16.6 us
    pallas_call x1, Pallas kernels, per_device(): pl.pallas_call(functools.partial(last_kernel, space, grp), out_shape=shap...  15.6 us
    pallas_call x1, Pallas kernels, per_device(): pl.pallas_call(functools.partial(main_kernel, span), out_shape=[shape((1,...  12.2 us
    unnamed x5, local copies, waits for them, and re-layouts  3.5 us

profile of v1, /device:TPU:1, one launch (start us, length us, event | category | flops | bytes accessed | tf_op | source)
XLA Modules:
  0.0 48.5 jit_solution(13166567874773197511)
XLA Ops:
  0.6 0.0 copy-start
  0.6 1.5 %copy.17.w_env_ref = bf16[256,64]{1,0:T(8,128)(2,1)} copy(bf16[256,64]{0,1:T(8,128)(2,1)} %param.24) | data formatting | bytes 65536 | tf_op args[9]
  2.1 0.0 copy-done
  2.1 0.7 %copy.18.w_val_ref = bf16[256,64]{1,0:T(8,128)(2,1)} copy(bf16[256,64]{0,1:T(8,128)(2,1)S(1)} %copy-done) | data formatting | bytes 65536 | tf_op args[10]
  2.9 16.6 %exchange_rows.1 = (bf16[8,256,128]{2,1,0:T(8,128)(2,1)}, bf16[256,256]{1,0:T(8,128)(2,1)}, bf16[256,256]{1,0:T(8,128)(2,1)}, f32[3,16,8,128]{3,2,1,0:T(8,128)},...) custom-call(f32[3,2048]{1,0:T(4,128)} %vec_ref.1, ...), custom_call_target="tpu_custom_call" | custom-call | tf_op jit(solution)/shard_map/exchange_rows/pallas_call | solution.py:345
  19.5 12.2 %edges.1 = (f32[1,256]{1,0:T(1,128)}, f32[3,256]{1,0:T(4,128)}, f32[8,8,128]{2,1,0:T(8,128)}) custom-call(s32[16,128]{1,0:T(8,128)} %bitcast.7, f32[3,16,8,128]{3,2,1,0:T(8,128)} %get-tuple-element.17.geo_ref, bf16[8,256,128]{2,1,0:T(8,128)(2,1)} %get-tuple-element.18.tab_ref, bf16[256,256]{1,0:T(8,128)(2,1)} %get-tuple-element.19.own_ref, ...), custom_call_target="tpu_custom_call" | custom-call | tf_op jit(solution)/shard_map/edges/pallas_call | solution.py:366
  31.7 15.6 %return_sums.1 = f32[3,256]{1,0:T(4,128)} custom-call(f32[8,8,128]{2,1,0:T(8,128)} %get-tuple-element.30.sums_ref, f32[3,256]{1,0:T(4,128)} %get-tuple-element.31.force_ref, s32[1,128]{1,0:T(1,128)} %rows_ref.3), custom_call_target="tpu_custom_call" | custom-call | tf_op jit(solution)/shard_map/return_sums/pallas_call | solution.py:390
  47.3 1.3 %copy.20 = f32[3,256]{1,0:T(4,128)} copy(f32[3,256]{1,0:T(4,128)} %return_sums.1) | data formatting | bytes 6144
Async XLA Ops:
  0.6 1.5 %copy-start = (bf16[256,64]{0,1:T(8,128)(2,1)S(1)}, bf16[256,64]{0,1:T(8,128)(2,1)}, u32[]{:S(2)}) copy-start(bf16[256,64]{0,1:T(8,128)(2,1)} %param.25) | copy-start | bytes 98308

commit v2 on v1

v2 whole, which is shorter than its diff:
```python
import functools
import math

import jax
import jax.numpy as jnp
from jax import lax
from jax.experimental import pallas as pl
from jax.experimental.pallas import tpu as pltpu
from jax.sharding import PartitionSpec as P

F32 = jnp.float32
BF16 = jnp.bfloat16
MESH = pl.DeviceIdType.MESH
OFFSETS = ((-1, -1), (-1, 0), (-1, 1), (0, -1), (0, 1), (1, -1), (1, 0), (1, 1))
STAGES = ((3, 4), (1, 6), (0, 2, 5, 7))
CUTOFF = 5.0
R3, R5, R15 = math.sqrt(3.0), math.sqrt(5.0), math.sqrt(15.0)
DEGREES = ((0,), (1, 2, 3), (4, 5, 6, 7, 8))
WIDTH = 256
EDGES = 2048
C = 64


def mm(lhs, rhs):
    return jnp.dot(lhs, rhs, preferred_element_type=F32)


def mm_nt(lhs, rhs):
    return lax.dot_general(lhs, rhs, (((1,), (1,)), ((), ())), preferred_element_type=F32)


def turned(block):
    return block.astype(F32).T.astype(BF16)


def sigmoid(x):
    return 0.5 + 0.5 * jnp.tanh(0.5 * x)


def onehot(row, count, first=0):
    ids = lax.broadcasted_iota(jnp.int16, (count, row.shape[1]), 0)
    own = (row - first).astype(jnp.int16)
    return jnp.where(ids == own, jnp.bfloat16(1.0), jnp.bfloat16(0.0))


def down(block):
    return jnp.sum(block, axis=0, keepdims=True)


def part(block, i):
    return block[i * C : (i + 1) * C]


def scaled(block, harm):
    return block if harm is None else block * harm


def harmonics(x, y, z):
    return [
        None, R3 * x, R3 * y, R3 * z,
        R15 * x * y, R15 * y * z, 0.5 * R5 * (3.0 * z * z - 1.0), R15 * x * z, 0.5 * R15 * (x * x - y * y),
    ]


def geometry(vec, centre, slot, mask, geo, dense):
    for i in range(3):
        for b in range(16):
            dense[i, b : b + 1, :] = vec[i : i + 1, b * 128 : (b + 1) * 128]
    real = mask[...] > 0
    vx, vy, vz = [jnp.where(real, dense[i], 1.0) for i in range(3)]
    dist = jnp.sqrt(vx * vx + vy * vy + vz * vz)
    inv = 1.0 / dist
    t = dist / CUTOFF
    angle = math.pi * t
    sin1, cos1 = jnp.sin(angle), jnp.cos(angle)
    scale = math.sqrt(2.0 / CUTOFF)
    sins, coss = [jnp.zeros_like(t), sin1], [jnp.ones_like(t), cos1]
    for n in range(2, 9):
        sins.append(2.0 * cos1 * sins[-1] - sins[-2])
        coss.append(2.0 * cos1 * coss[-1] - coss[-2])
    for n in range(1, 9):
        radial = scale * sins[n] * inv
        geo[0, :, n - 1, :] = radial
        geo[1, :, n - 1, :] = (scale * n * math.pi / CUTOFF * coss[n] - radial) * inv
    t2 = t * t
    t4 = t2 * t2
    t5, t6, t7, t8 = t4 * t, t4 * t2, t4 * t2 * t, t4 * t4
    geo[2, :, 0, :] = vx * inv
    geo[2, :, 1, :] = vy * inv
    geo[2, :, 2, :] = vz * inv
    geo[2, :, 3, :] = inv
    geo[2, :, 4, :] = 1.0 - 28.0 * t6 + 48.0 * t7 - 21.0 * t8
    geo[2, :, 5, :] = (336.0 * t6 - 168.0 * t5 - 168.0 * t7) / CUTOFF
    geo[2, :, 6, :] = jnp.where(real, centre[...], -1).astype(F32)
    geo[2, :, 7, :] = jnp.where(real, slot[...], -1).astype(F32)


def kernel(
    space, grp, span,
    vec_in, feat_in, centre_in, slot_in, mask_in, rows_in, w_radial_in, w_centre_in, w_nbr_in, w_env_in, w_val_in,
    w_mix_in, w_scal_in, w_read_in, w_out_in,
    energy_ref, force_ref,
    vec, feat, centre, slot, mask, send_rows, w_radial, w_centre, w_nbr, wevt, w_mix, w_scal, w_read, w_out,
    outgoing, tab, near, geo, dense, wr, wrhl, wev, wmixt, wscalt, wreadt, wout,
    lat_s, act_s, slope_s, wv_s, back_s, vbar_s, hbar_s, en_s, env_s, envh_s, fsum, csum, leaving, landed,
    in_sem, send_sem, recv_sem, send_sem2, recv_sem2,
):
    wide = span // 128
    chunks = EDGES // span
    me_s, me_g = lax.axis_index("space"), lax.axis_index("grp")
    peers = [(lax.rem(me_s + a + space, space), lax.rem(me_g + b + grp, grp)) for a, b in OFFSETS]
    barrier = pltpu.get_barrier_semaphore()
    for peer in peers:
        pl.semaphore_signal(barrier, inc=1, device_id=peer, device_id_type=MESH)
    pairs = [
        (feat_in, feat), (w_nbr_in, w_nbr), (rows_in, send_rows), (w_centre_in, w_centre), (vec_in, vec), (centre_in, centre),
        (slot_in, slot), (mask_in, mask), (w_radial_in, w_radial), (w_env_in, wevt.at[0:C]), (w_val_in, wevt.at[C : 2 * C]),
        (w_mix_in, w_mix), (w_scal_in, w_scal), (w_read_in, w_read), (w_out_in, w_out),
    ]
    loads = [pltpu.make_async_copy(a, b, in_sem.at[i]) for i, (a, b) in enumerate(pairs)]
    for load in loads:
        load.start()
    for load in loads[:3]:
        load.wait()
    own = mm(feat[...], w_nbr[...]).T.astype(BF16)
    near[:, 0:WIDTH] = own
    outgoing[...] = mm(own, onehot(send_rows[...], WIDTH)).astype(BF16)
    pl.semaphore_wait(barrier, 8)

    def remote(c, source, landing, sends, receives):
        return pltpu.make_async_remote_copy(
            src_ref=source,
            dst_ref=landing.at[7 - c],
            send_sem=sends.at[c],
            recv_sem=receives.at[7 - c],
            device_id=peers[c],
            device_id_type=MESH,
        )

    copies = [remote(c, outgoing, tab, send_sem, recv_sem) for c in range(8)]
    for stage in STAGES:
        for c in stage:
            copies[c].start()
    for load in loads[3:]:
        load.wait()
    near[:, WIDTH:] = mm(feat[...], w_centre[...]).T.astype(BF16)
    geometry(vec, centre, slot, mask, geo, dense)
    high = w_radial[...].astype(BF16).astype(F32)
    low = w_radial[...] - high
    stacked = jnp.concatenate([high, low, high, jnp.zeros((104, WIDTH), F32)], axis=0)
    wr[...] = stacked.T[:, :32].astype(BF16)
    wrhl[...] = jnp.concatenate([high, low], axis=0).astype(BF16)

    def rows(group, j):
        return jnp.concatenate([geo[group, wide * j + i] for i in range(wide)], axis=1)

    def fields(j):
        block = rows(2, j)
        return [block[i : i + 1] for i in range(8)]

    def index(row):
        return row.astype(jnp.int32)

    for j in range(chunks):
        radial = rows(0, j)
        top = radial.astype(BF16).astype(F32)
        terms = jnp.concatenate([top, top, radial - top, jnp.zeros_like(top)], axis=0).astype(BF16)
        marks = fields(j)
        hot = jnp.concatenate([onehot(index(marks[7]), WIDTH), onehot(index(marks[6]), WIDTH)], axis=0)
        act_s[j] = mm(near[...], hot) + mm(wr[...], terms)

    wev[...] = turned(wevt[...])
    wmixt[...] = turned(w_mix[...])
    padded = jnp.concatenate([w_scal[...].astype(F32), jnp.zeros((C, WIDTH), F32)], axis=0)
    wscalt[...] = padded.T[:, : 3 * C].astype(BF16)
    wreadt[...] = turned(w_read[...])
    wout[...] = jnp.broadcast_to(w_out[...], (128, WIDTH)).T

    def gathered(j, stage):
        slots = index(fields(j)[7])
        hot = jnp.concatenate([onehot(slots, 128, WIDTH + 128 * c) for c in stage], axis=0)
        return act_s[j] + mm(jnp.concatenate([tab[c] for c in stage], axis=1), hot)

    for stage in STAGES[:2]:
        for c in stage:
            copies[7 - c].wait_recv()
        for j in range(chunks):
            act_s[j] = gathered(j, stage)
    for c in STAGES[2]:
        copies[7 - c].wait_recv()

    for j in range(chunks):
        x, y, z, _, envelope, _, centres, _ = fields(j)
        lifted = gathered(j, STAGES[2])
        gate = sigmoid(lifted)
        active = lifted * gate
        act_s[j] = active
        slope_s[j] = gate + active * (1.0 - gate)
        latent = (active * envelope).astype(BF16)
        lat_s[j] = latent
        wv = mm(wevt[...], latent)
        wv_s[j] = wv
        weights = wv[:C]
        harm = harmonics(x, y, z)
        spread = jnp.concatenate([scaled(weights, harm[i]).astype(BF16) for i in range(9)], axis=0)
        term = mm_nt(spread, onehot(index(centres), WIDTH))
        env_s[...] = term if j == 0 else env_s[...] + term
    envh_s[...] = (env_s[...] * 0.125).astype(BF16)

    for j in range(chunks):
        x, y, z, _, _, _, centres, _ = fields(j)
        hot = onehot(index(centres), WIDTH)
        harm = harmonics(x, y, z)
        local = mm(envh_s[...], hot)
        values = wv_s[j, C:]
        invariants = []
        for degree in DEGREES:
            whole = None
            for i in degree:
                term = scaled(part(local, i), harm[i])
                whole = term if whole is None else whole + term
            invariants.append(whole)
        scal = jnp.concatenate([(q * values).astype(BF16) for q in invariants], axis=0)
        latent = lat_s[j]
        update = mm(wmixt[...], latent) + mm(wscalt[...], scal)
        gate = sigmoid(update)
        active = update * gate
        slope = gate + active * (1.0 - gate)
        mixed = (latent.astype(F32) + active).astype(BF16)
        hidden = mm(wreadt[...], mixed)
        gate_h = sigmoid(hidden)
        active_h = hidden * gate_h
        out = jnp.concatenate([wout[...]] * wide, axis=1)
        en_s[j] = down(active_h * out)
        hidden_bar = (out * (gate_h + active_h * (1.0 - gate_h))).astype(BF16)
        mixed_bar = mm(w_read[...], hidden_bar).astype(BF16).astype(F32)
        update_bar = (mixed_bar * slope).astype(BF16)
        back_s[j] = mixed_bar + mm(w_mix[...], update_bar)
        scal_bar = mm(w_scal[...], update_bar)
        values_bar = None
        locals_bar, harm_bar = [], []
        for level, degree in enumerate(DEGREES):
            bar = part(scal_bar, level)
            term = bar * invariants[level]
            values_bar = term if values_bar is None else values_bar + term
            inner = bar * values
            for i in degree:
                locals_bar.append(scaled(inner, harm[i]).astype(BF16))
                if i:
                    harm_bar.append(down(part(local, i) * inner))
        vbar_s[j] = values_bar.astype(BF16)
        hbar_s[j] = jnp.concatenate(harm_bar, axis=0)
        term = mm_nt(jnp.concatenate(locals_bar, axis=0), hot)
        env_s[...] = term if j == 0 else env_s[...] + term
    envh_s[...] = (env_s[...] * 0.125).astype(BF16)

    for j in range(chunks):
        x, y, z, inv, envelope, slope_env, centres, slots = fields(j)
        slots = index(slots)
        hot = onehot(index(centres), WIDTH)
        harm = harmonics(x, y, z)
        spread_bar = mm(envh_s[...], hot)
        weights = wv_s[j, :C]
        weights_bar = part(spread_bar, 0)
        for i in range(1, 9):
            weights_bar = weights_bar + part(spread_bar, i) * harm[i]
        harm_bar = hbar_s[j]
        bars = [None] + [harm_bar[i - 1 : i] + down(part(spread_bar, i) * weights) for i in range(1, 9)]
        wv_bar = jnp.concatenate([weights_bar.astype(BF16), vbar_s[j]], axis=0)
        latent_bar = back_s[j] + mm(wev[...], wv_bar)
        envelope_bar = down(latent_bar * act_s[j])
        lifted_bar = (latent_bar * envelope * slope_s[j]).astype(BF16)
        radial_bar = mm(wrhl[...], lifted_bar)
        dist_bar = down((radial_bar[:8] + radial_bar[8:]) * rows(1, j)) + envelope_bar * slope_env
        ux = R3 * bars[1] + R15 * (y * bars[4] + z * bars[7] + x * bars[8])
        uy = R3 * bars[2] + R15 * (x * bars[4] + z * bars[5] - y * bars[8])
        uz = R3 * bars[3] + R15 * (y * bars[5] + x * bars[7]) + 3.0 * R5 * z * bars[6]
        along = dist_bar - (x * ux + y * uy + z * uz) * inv
        grads = jnp.concatenate([ux * inv + x * along, uy * inv + y * along, uz * inv + z * along, en_s[j]], axis=0)
        top = grads.astype(BF16).astype(F32)
        both = jnp.concatenate([top, grads - top], axis=0)
        block = lax.shift_right_arithmetic(slots, 7)
        low_hot = onehot(lax.bitwise_and(slots, 127), 128)
        split = jnp.concatenate([jnp.where(block == h, both, 0.0) for h in range(10)], axis=0).astype(BF16)
        term, own_term = mm_nt(split, low_hot), mm_nt(both.astype(BF16), hot)
        fsum[...] = term if j == 0 else fsum[...] + term
        csum[...] = own_term if j == 0 else csum[...] + own_term

    for c in range(8):
        first = 16 + 8 * c
        leaving[c, 0:4] = fsum[first : first + 4] + fsum[first + 4 : first + 8]
        leaving[c, 4:8] = jnp.zeros((4, 128), F32)
    returns = [remote(c, leaving.at[c], landed, send_sem2, recv_sem2) for c in range(8)]
    for copy in returns:
        copy.start()
    centre_sum = csum[0:4] + csum[4:8]
    energy_ref[...] = centre_sum[3:4]
    own_sum = jnp.concatenate([fsum[0:4] + fsum[4:8], fsum[8:12] + fsum[12:16]], axis=1)
    hot = onehot(send_rows[...], WIDTH)
    for copy in returns:
        copy.wait_recv()
    total = landed[0]
    for c in range(1, 8):
        total = total + landed[c]
    top = total.astype(BF16).astype(F32)
    away = mm_nt(jnp.concatenate([top, total - top], axis=0).astype(BF16), hot)
    force_ref[...] = (centre_sum - own_sum)[0:3] - (away[0:3] + away[8:11])
    for copy in copies + returns:
        copy.wait_send()


def per_device(
    space, grp,
    rel_vec, atom_feat, centre, nbr_slot, edge_mask, send_rows, w_radial, w_centre, w_nbr, w_env, w_val, w_mix, w_scal,
    w_read, w_out,
):
    span = 1024
    chunks = EDGES // span
    shape = jax.ShapeDtypeStruct
    vm = pltpu.VMEM
    energy, forces = pl.pallas_call(
        functools.partial(kernel, space, grp, span),
        out_shape=[shape((1, WIDTH), F32), shape((3, WIDTH), F32)],
        in_specs=[pl.BlockSpec(memory_space=pl.ANY)] * 15,
        out_specs=[pl.BlockSpec(memory_space=pltpu.VMEM)] * 2,
        scratch_shapes=[
            vm((3, EDGES), F32), vm((WIDTH, WIDTH), BF16), vm((16, 128), jnp.int32), vm((16, 128), jnp.int32),
            vm((16, 128), jnp.int32), vm((1, 128), jnp.int32), vm((8, WIDTH), F32), vm((WIDTH, WIDTH), BF16),
            vm((WIDTH, WIDTH), BF16), vm((2 * C, WIDTH), BF16), vm((WIDTH, WIDTH), BF16), vm((3 * C, WIDTH), BF16),
            vm((WIDTH, WIDTH), BF16), vm((1, WIDTH), F32),
            vm((WIDTH, 128), BF16), vm((8, WIDTH, 128), BF16), vm((WIDTH, 2 * WIDTH), BF16), vm((3, 16, 8, 128), F32),
            vm((3, 16, 128), F32), vm((WIDTH, 32), BF16), vm((16, WIDTH), BF16), vm((WIDTH, 2 * C), BF16),
            vm((WIDTH, WIDTH), BF16), vm((WIDTH, 3 * C), BF16), vm((WIDTH, WIDTH), BF16), vm((WIDTH, 128), F32),
            vm((chunks, WIDTH, span), BF16), vm((chunks, WIDTH, span), F32), vm((chunks, WIDTH, span), F32),
            vm((chunks, 2 * C, span), F32), vm((chunks, WIDTH, span), F32), vm((chunks, C, span), BF16),
            vm((chunks, 8, span), F32), vm((chunks, 1, span), F32), vm((9 * C, WIDTH), F32), vm((9 * C, WIDTH), BF16),
            vm((80, 128), F32), vm((8, WIDTH), F32), vm((8, 8, 128), F32), vm((8, 8, 128), F32),
            pltpu.SemaphoreType.DMA((15,)), pltpu.SemaphoreType.DMA((8,)), pltpu.SemaphoreType.DMA((8,)),
            pltpu.SemaphoreType.DMA((8,)), pltpu.SemaphoreType.DMA((8,)),
        ],
        compiler_params=pltpu.CompilerParams(collective_id=0, has_side_effects=True, vmem_limit_bytes=56 * 1024 * 1024),
        name="layer",
    )(
        rel_vec, atom_feat, centre.reshape(16, 128), nbr_slot.reshape(16, 128), edge_mask.reshape(16, 128), send_rows, w_radial,
        w_centre, w_nbr, w_env.T, w_val.T, w_mix, w_scal, w_read, w_out.reshape(1, WIDTH),
    )
    return (energy.reshape(WIDTH), forces)


def solution(mesh):
    edges = P(("space", "grp"))
    placed = (
        P(None, ("space", "grp")), P(("space", "grp"), None), edges, edges, edges, P(("space", "grp"), None),
    ) + (P(),) * 9
    return jax.shard_map(
        functools.partial(per_device, mesh.shape["space"], mesh.shape["grp"]),
        mesh=mesh,
        in_specs=placed,
        out_specs=(edges, P(None, ("space", "grp"))),
        check_vma=False,
    )
```

time: 48.9 us -> 34.3 us (0.70)
  Pallas kernels: 44.4 us -> 31.7 us
  local copies, waits for them, and re-layouts: 3.5 us -> 1.79 us
    pallas_call x3 -> x1, Pallas kernels: 44.4 us -> 31.7 us  [per_device(): pl.pallas_call(functools.partial(kernel, space, grp, span), out_shape=[sh...]
    unnamed x5 -> x6, local copies, waits for them, and re-layouts: 3.5 us -> 1.79 us
where the time goes in v2:
time: 34.3 us; the launch traced here: 34.2 us
  Pallas kernels  31.7 us (92%)
  local copies, waits for them, and re-layouts  1.79 us (5%)
  between operations  0.66 us (2%)
    pallas_call x1, Pallas kernels, per_device(): pl.pallas_call(functools.partial(kernel, space, grp, span), out_shape=[sh...  31.7 us
    unnamed x6, local copies, waits for them, and re-layouts  1.79 us

profile of v2, /device:TPU:1, one launch (start us, length us, event | category | flops | bytes accessed | tf_op | source)
XLA Modules:
  0.0 34.2 jit_solution(16824268272620499690)
XLA Ops:
  0.6 31.7 %layer.1 = (f32[1,256]{1,0:T(1,128)}, f32[3,256]{1,0:T(4,128)}) custom-call(f32[3,2048]{1,0:T(4,128)} %vec_in.1, bf16[256,256]{1,0:T(8,128)(2,1)} %feat_in.1, s32[16,128]{1,0:T(8,128)} %bitcast.9, s32[16,128]{1,0:T(8,128)} %bitcast.10, s32[16,128]{1,0:T(8,128)} %bitcast.11, s32[1,128]{1,0:T(1,128)} %rows_in.1, f32[8,256]{1,0:T(8,128)} %w_radial_in.1, ...), custom_call_target="tpu_custom_call" | custom-call | tf_op jit(solution)/shard_map/layer/pallas_call | solution.py:321
  32.4 0.0 copy-start
  32.4 0.0 copy-start.1
  32.4 0.6 %copy-done.1 = f32[1,256]{1,0:T(1,128)S(1)} copy-done((f32[1,256]{1,0:T(1,128)S(1)}, f32[1,256]{1,0:T(1,128)}, u32[]{:S(2)}) %copy-start.1) | copy-done | bytes 1048
  33.0 0.6 %copy.19 = f32[256]{0:T(256)} copy(f32[256]{0:T(256)S(1)} %bitcast.12) | data formatting | bytes 2048
  33.6 0.0 copy-done
  33.6 0.6 %copy.20 = f32[3,256]{1,0:T(4,128)} copy(f32[3,256]{1,0:T(4,128)S(1)} %copy-done) | data formatting | bytes 6144
Async XLA Ops:
  32.4 1.2 %copy-start = (f32[3,256]{1,0:T(4,128)S(1)}, f32[3,256]{1,0:T(4,128)}, u32[]{:S(2)}) copy-start(f32[3,256]{1,0:T(4,128)} %get-tuple-element.9) | copy-start | bytes 9220
  32.4 0.6 %copy-start.1 = (f32[1,256]{1,0:T(1,128)S(1)}, f32[1,256]{1,0:T(1,128)}, u32[]{:S(2)}) copy-start(f32[1,256]{1,0:T(1,128)} %get-tuple-element.4) | copy-start | bytes 3076

commit v3 on v2

v3 whole, which is shorter than its diff:
```python
import functools
import math

import jax
import jax.numpy as jnp
from jax import lax
from jax.experimental import pallas as pl
from jax.experimental.pallas import tpu as pltpu
from jax.sharding import PartitionSpec as P

F32 = jnp.float32
BF16 = jnp.bfloat16
MESH = pl.DeviceIdType.MESH
OFFSETS = ((-1, -1), (-1, 0), (-1, 1), (0, -1), (0, 1), (1, -1), (1, 0), (1, 1))
STAGES = ((0, 1), (2, 3), (4, 5, 6, 7))
BACK = (0, 1, 3, 2, 5, 4, 7, 6)
CUTOFF = 5.0
R3, R5, R15 = math.sqrt(3.0), math.sqrt(5.0), math.sqrt(15.0)
DEGREES = ((0,), (1, 2, 3), (4, 5, 6, 7, 8))
WIDTH = 256
EDGES = 2048
C = 64


def mm(lhs, rhs):
    return jnp.dot(lhs, rhs, preferred_element_type=F32)


def mm_nt(lhs, rhs):
    return lax.dot_general(lhs, rhs, (((1,), (1,)), ((), ())), preferred_element_type=F32)


def turned(block):
    return block.astype(F32).T.astype(BF16)


def gated(half):
    rise = 1.0 + jnp.tanh(half)
    active = half * rise
    return active, (rise + active * (2.0 - rise)).astype(BF16)


def halved(block):
    return (0.5 * block.astype(F32)).astype(BF16)


def pipeline(steps):
    waiting, running = list(steps), []
    while waiting or running:
        if waiting:
            running.append(waiting.pop(0))
        running = [step for step in running if next(step, "end") != "end"]


def onehot(row, count, first=0):
    ids = lax.broadcasted_iota(jnp.int16, (count, row.shape[1]), 0)
    own = (row - first).astype(jnp.int16)
    return jnp.where(ids == own, jnp.bfloat16(1.0), jnp.bfloat16(0.0))


def down(block):
    return jnp.sum(block, axis=0, keepdims=True)


def part(block, i):
    return block[i * C : (i + 1) * C]


def scaled(block, harm):
    return block if harm is None else block * harm


def harmonics_exact(x, y, z):
    return [
        None, R3 * x, R3 * y, R3 * z,
        R15 * x * y, R15 * y * z, 0.5 * R5 * (3.0 * z * z - 1.0), R15 * x * z, 0.5 * R15 * (x * x - y * y),
    ]


def harmonics(x, y, z):
    return [None] + [harm.astype(BF16) for harm in harmonics_exact(x, y, z)[1:]]


def geometry(vec, centre, slot, mask, geo, dense):
    for i in range(3):
        for b in range(16):
            dense[i, b : b + 1, :] = vec[i : i + 1, b * 128 : (b + 1) * 128]
    real = mask[...] > 0
    vx, vy, vz = [jnp.where(real, dense[i], 1.0) for i in range(3)]
    dist = jnp.sqrt(vx * vx + vy * vy + vz * vz)
    inv = 1.0 / dist
    t = dist / CUTOFF
    angle = math.pi * t
    sin1, cos1 = jnp.sin(angle), jnp.cos(angle)
    scale = math.sqrt(2.0 / CUTOFF)
    sins, coss = [jnp.zeros_like(t), sin1], [jnp.ones_like(t), cos1]
    for n in range(2, 9):
        sins.append(2.0 * cos1 * sins[-1] - sins[-2])
        coss.append(2.0 * cos1 * coss[-1] - coss[-2])
    for n in range(1, 9):
        radial = scale * sins[n] * inv
        geo[0, :, n - 1, :] = radial
        geo[1, :, n - 1, :] = (scale * n * math.pi / CUTOFF * coss[n] - radial) * inv
    t2 = t * t
    t4 = t2 * t2
    t5, t6, t7, t8 = t4 * t, t4 * t2, t4 * t2 * t, t4 * t4
    geo[2, :, 0, :] = vx * inv
    geo[2, :, 1, :] = vy * inv
    geo[2, :, 2, :] = vz * inv
    geo[2, :, 3, :] = inv
    geo[2, :, 4, :] = 1.0 - 28.0 * t6 + 48.0 * t7 - 21.0 * t8
    geo[2, :, 5, :] = (336.0 * t6 - 168.0 * t5 - 168.0 * t7) / CUTOFF
    geo[2, :, 6, :] = jnp.where(real, centre[...], -1).astype(F32)
    geo[2, :, 7, :] = jnp.where(real, slot[...], -1).astype(F32)


def kernel(
    space, grp, span,
    vec_in, feat_in, centre_in, slot_in, mask_in, rows_in, w_radial_in, w_centre_in, w_nbr_in, w_env_in, w_val_in,
    w_mix_in, w_scal_in, w_read_in, w_out_in,
    result_ref, rest_ref,
    vec, feat, centre, slot, mask, send_rows, w_radial, w_centre, w_nbr, wevt, w_mix, w_scal, w_read, w_out,
    outgoing, tab, near, geo, dense, wr, wrhl, wev, wmixt, wreadt, wout, woutf,
    hot_s, far_s, lat_s, actb_s, act_s, slope_s, wv_s, back_s, vbar_s, hbar_s, en_s, env_s, envh_s, fsum, leaving, landed,
    in_sem, send_sem, recv_sem, send_sem2, recv_sem2,
):
    wide = span // 128
    chunks = EDGES // span
    me_s, me_g = lax.axis_index("space"), lax.axis_index("grp")
    peers = [(lax.rem(me_s + a + space, space), lax.rem(me_g + b + grp, grp)) for a, b in OFFSETS]
    barrier = pltpu.get_barrier_semaphore()
    for peer in peers:
        pl.semaphore_signal(barrier, inc=1, device_id=peer, device_id_type=MESH)
    pairs = [
        (feat_in, feat), (w_nbr_in, w_nbr), (rows_in, send_rows), (w_centre_in, w_centre), (vec_in, vec), (centre_in, centre),
        (slot_in, slot), (mask_in, mask), (w_radial_in, w_radial), (w_env_in, wevt.at[0:C]), (w_val_in, wevt.at[C : 2 * C]),
        (w_mix_in, w_mix), (w_scal_in, w_scal), (w_read_in, w_read), (w_out_in, w_out),
    ]
    loads = [pltpu.make_async_copy(a, b, in_sem.at[i]) for i, (a, b) in enumerate(pairs)]
    for load in loads:
        load.start()
    for load in loads[:3]:
        load.wait()
    own = (0.5 * mm(feat[...], w_nbr[...])).T.astype(BF16)
    near[:, 0:WIDTH] = own
    outgoing[...] = mm(own, onehot(send_rows[...], WIDTH)).astype(BF16)
    pl.semaphore_wait(barrier, 8)

    mate = 1 - 2 * lax.rem(me_g, 2)
    steps = ((0, mate), (0, -mate), (-1, 0), (1, 0), (-1, mate), (1, mate), (-1, -mate), (1, -mate))
    partners = [(lax.rem(me_s + a + space, space), lax.rem(me_g + b + grp, grp)) for a, b in steps]
    flat = [3 * (a + 1) + b + 1 for a, b in steps]
    blocks = [f - jnp.where(f > 4, 1, 0) for f in flat]

    def remote(source, target, sends, receives, device):
        return pltpu.make_async_remote_copy(
            src_ref=source, dst_ref=target, send_sem=sends, recv_sem=receives, device_id=device, device_id_type=MESH
        )

    def sent(role):
        return remote(outgoing, tab.at[BACK[role]], send_sem.at[role], recv_sem.at[BACK[role]], partners[role])

    def passed(role):
        return remote(tab.at[role - 2], tab.at[role], send_sem.at[role], recv_sem.at[role], partners[0])

    copies = {role: sent(role) for role in (3, 2, 7, 6, 1, 0)}
    for role in (3, 2, 7, 6, 1, 0):
        copies[role].start()
    for load in loads[3:]:
        load.wait()
    near[:, WIDTH:] = (0.5 * mm(feat[...], w_centre[...])).T.astype(BF16)
    geometry(vec, centre, slot, mask, geo, dense)
    half_radial = 0.5 * w_radial[...]
    high = half_radial.astype(BF16).astype(F32)
    low = half_radial - high
    stacked = jnp.concatenate([high, low, high, jnp.zeros((104, WIDTH), F32)], axis=0)
    wr[...] = stacked.T[:, :32].astype(BF16)
    wrhl[...] = jnp.concatenate([high, low], axis=0).astype(BF16)

    def rows(group, j):
        return jnp.concatenate([geo[group, wide * j + i] for i in range(wide)], axis=1)

    def fields(j):
        block = rows(2, j)
        return [block[i : i + 1] for i in range(8)]

    def index(row):
        return row.astype(jnp.int32)

    for j in range(chunks):
        radial = rows(0, j)
        top = radial.astype(BF16).astype(F32)
        terms = jnp.concatenate([top, top, radial - top, jnp.zeros_like(top)], axis=0).astype(BF16)
        marks = fields(j)
        hot_s[j] = onehot(index(marks[6]), WIDTH)
        hot = jnp.concatenate([onehot(index(marks[7]), WIDTH), hot_s[j]], axis=0)
        act_s[j] = mm(near[...], hot) + mm(wr[...], terms)

    wev[...] = turned(wevt[...])
    w_mix[...] = halved(w_mix[...])
    w_scal[...] = halved(w_scal[...])
    w_read[...] = halved(w_read[...])
    wmixt[:, 0:WIDTH] = turned(w_mix[...])
    padded = jnp.concatenate([w_scal[...].astype(F32), jnp.zeros((C, WIDTH), F32)], axis=0)
    wmixt[:, WIDTH:] = padded.T.astype(BF16)
    wreadt[...] = turned(w_read[...])
    woutf[...] = jnp.broadcast_to(w_out[...], (128, WIDTH)).T
    wout[...] = woutf[...].astype(BF16)
    for j in range(chunks):
        slots = index(fields(j)[7])
        far_s[j] = jnp.concatenate([onehot(slots, 128, WIDTH + 128 * c) for c in blocks], axis=0)

    def add(total, term, j):
        total[...] = term if j == 0 else total[...] + term

    def gathered(j, stage):
        hot = far_s[j, 128 * stage[0] : 128 * (stage[-1] + 1)]
        return act_s[j] + mm(jnp.concatenate([tab[role] for role in stage], axis=1), hot)

    for role in (2, 3):
        copies[BACK[role]].wait_recv()
        copies[role + 2] = passed(role + 2)
        copies[role + 2].start()
    for role in (0, 1):
        copies[role].wait_recv()
    for stage in STAGES[:2]:
        for j in range(chunks):
            act_s[j] = gathered(j, stage)
    for role in (4, 5):
        copies[role].wait_recv()
    for role in (6, 7):
        copies[BACK[role]].wait_recv()

    def forward(j):
        x, y, z, _, envelope, _, _, _ = fields(j)
        lifted = gathered(j, STAGES[2])
        yield
        active, slope = gated(lifted)
        actb_s[j] = active.astype(BF16)
        slope_s[j] = slope
        latent = (active * envelope).astype(BF16)
        lat_s[j, 0:WIDTH] = latent
        yield
        wv = mm(wevt[...], latent).astype(BF16)
        wv_s[j] = wv
        yield
        weights = wv[:C]
        harm = harmonics(x, y, z)
        spread = jnp.concatenate([scaled(weights, harm[i]) for i in range(9)], axis=0)
        yield
        add(env_s, mm_nt(spread, hot_s[j]), j)

    def middle(j):
        x, y, z, _, _, _, _, _ = fields(j)
        hot = hot_s[j]
        exact, harm = harmonics_exact(x, y, z), harmonics(x, y, z)
        local = mm(envh_s[...], hot)
        yield
        values = wv_s[j, C:]
        invariants = []
        for degree in DEGREES:
            whole = None
            for i in degree:
                term = scaled(part(local, i), exact[i])
                whole = term if whole is None else whole + term
            invariants.append(whole.astype(BF16))
        lat_s[j, WIDTH:] = jnp.concatenate([q * values for q in invariants] + [jnp.zeros_like(values)], axis=0)
        yield
        update = mm(wmixt[...], lat_s[j])
        yield
        active, slope = gated(update)
        mixed = lat_s[j, 0:WIDTH] + active.astype(BF16)
        yield
        hidden = mm(wreadt[...], mixed)
        yield
        active_h, slope_h = gated(hidden)
        en_s[j] = down(active_h * jnp.concatenate([woutf[...]] * wide, axis=1))
        hidden_bar = jnp.concatenate([wout[...]] * wide, axis=1) * slope_h
        yield
        mixed_bar = mm(w_read[...], hidden_bar)
        yield
        mixed_bar = mixed_bar.astype(BF16)
        update_bar = mixed_bar * slope
        yield
        back_s[j] = mixed_bar.astype(F32) + mm(w_mix[...], update_bar)
        scal_f = mm(w_scal[...], update_bar)
        scal_bar = scal_f.astype(BF16)
        yield
        values_bar = None
        locals_bar, products = [], []
        for level, degree in enumerate(DEGREES):
            bar = part(scal_bar, level)
            term = bar * invariants[level]
            values_bar = term if values_bar is None else values_bar + term
            inner_f = part(scal_f, level) * values.astype(F32)
            inner = inner_f.astype(BF16)
            for i in degree:
                locals_bar.append(scaled(inner, harm[i]))
                if i:
                    products.append(down(part(local, i) * inner_f))
        vbar_s[j] = values_bar
        hbar_s[j] = jnp.concatenate(products, axis=0)
        yield
        add(env_s, mm_nt(jnp.concatenate(locals_bar, axis=0), hot), j)

    def backward(j):
        x, y, z, inv, envelope, slope_env, centres, slots = fields(j)
        slots, centres = index(slots), index(centres)
        hot = hot_s[j]
        harm = harmonics_exact(x, y, z)
        spread_bar = mm(envh_s[...], hot)
        yield
        weights = wv_s[j, :C].astype(F32)
        weights_bar = part(spread_bar, 0)
        for i in range(1, 9):
            weights_bar = weights_bar + part(spread_bar, i) * harm[i]
        products = [down(part(spread_bar, i) * weights) for i in range(1, 9)]
        wv_bar = jnp.concatenate([weights_bar.astype(BF16), vbar_s[j]], axis=0)
        yield
        latent_f = back_s[j] + mm(wev[...], wv_bar)
        latent_bar = latent_f.astype(BF16)
        harm_bar = hbar_s[j] + jnp.concatenate(products, axis=0)
        bars = [None] + [harm_bar[i : i + 1] for i in range(8)]
        yield
        envelope_bar = down(latent_f * actb_s[j].astype(F32))
        lifted_bar = latent_bar * envelope.astype(BF16) * slope_s[j]
        yield
        radial_bar = mm(wrhl[...], lifted_bar)
        yield
        dist_bar = down((radial_bar[:8] + radial_bar[8:]) * rows(1, j)) + envelope_bar * slope_env
        ux = R3 * bars[1] + R15 * (y * bars[4] + z * bars[7] + x * bars[8])
        uy = R3 * bars[2] + R15 * (x * bars[4] + z * bars[5] - y * bars[8])
        uz = R3 * bars[3] + R15 * (y * bars[5] + x * bars[7]) + 3.0 * R5 * z * bars[6]
        along = dist_bar - (x * ux + y * uy + z * uz) * inv
        grads = jnp.concatenate([ux * inv + x * along, uy * inv + y * along, uz * inv + z * along, en_s[j]], axis=0)
        top = grads.astype(BF16).astype(F32)
        both = jnp.concatenate([top, grads - top], axis=0)
        split = [jnp.where(lax.shift_right_arithmetic(slots, 7) == h, both, 0.0) for h in range(10)]
        split += [jnp.where(lax.shift_right_arithmetic(centres, 7) == h, both, 0.0) for h in range(2)]
        low = jnp.concatenate([onehot(lax.bitwise_and(row, 127), 128) for row in (slots, centres)], axis=0)
        yield
        add(fsum, mm_nt(jnp.concatenate(split, axis=0).astype(BF16), low), j)

    pipeline(forward(j) for j in range(chunks))
    envh_s[...] = (env_s[...] * 0.125).astype(BF16)
    pipeline(middle(j) for j in range(chunks))
    envh_s[...] = (env_s[...] * 0.125).astype(BF16)
    pipeline(backward(j) for j in range(chunks))

    def summed(first, side):
        return fsum[first : first + 4, 128 * side : 128 * side + 128] + fsum[first + 4 : first + 8, 128 * side : 128 * side + 128]

    for c in range(8):
        leaving[c, 0:4] = summed(16 + 8 * c, 0)
        leaving[c, 4:8] = jnp.zeros((4, 128), F32)
    returns = [remote(leaving.at[c], landed.at[7 - c], send_sem2.at[c], recv_sem2.at[7 - c], peers[c]) for c in range(8)]
    for c in (0, 2, 5, 7, 1, 6, 3, 4):
        returns[c].start()
    centre_sum = jnp.concatenate([summed(80, 1), summed(88, 1)], axis=1)
    own_sum = jnp.concatenate([summed(0, 0), summed(8, 0)], axis=1)
    hot = onehot(send_rows[...], WIDTH)
    for copy in returns:
        copy.wait_recv()
    total = landed[0]
    for c in range(1, 8):
        total = total + landed[c]
    top = total.astype(BF16).astype(F32)
    away = mm_nt(jnp.concatenate([top, total - top], axis=0).astype(BF16), hot)
    result_ref[...] = centre_sum
    rest_ref[0:3] = -own_sum[0:3] - (away[0:3] + away[8:11])
    rest_ref[3:4] = jnp.zeros((1, WIDTH), F32)
    for copy in list(copies.values()) + returns:
        copy.wait_send()


def per_device(
    space, grp,
    rel_vec, atom_feat, centre, nbr_slot, edge_mask, send_rows, w_radial, w_centre, w_nbr, w_env, w_val, w_mix, w_scal,
    w_read, w_out,
):
    span = 512
    chunks = EDGES // span
    shape = jax.ShapeDtypeStruct
    vm = pltpu.VMEM
    result = pl.pallas_call(
        functools.partial(kernel, space, grp, span),
        out_shape=[vm((4, WIDTH), F32)] * 2,
        in_specs=[pl.BlockSpec(memory_space=pl.ANY)] * 15,
        out_specs=[pl.BlockSpec(memory_space=pltpu.VMEM)] * 2,
        scratch_shapes=[
            vm((3, EDGES), F32), vm((WIDTH, WIDTH), BF16), vm((16, 128), jnp.int32), vm((16, 128), jnp.int32),
            vm((16, 128), jnp.int32), vm((1, 128), jnp.int32), vm((8, WIDTH), F32), vm((WIDTH, WIDTH), BF16),
            vm((WIDTH, WIDTH), BF16), vm((2 * C, WIDTH), BF16), vm((WIDTH, WIDTH), BF16), vm((3 * C, WIDTH), BF16),
            vm((WIDTH, WIDTH), BF16), vm((1, WIDTH), F32),
            vm((WIDTH, 128), BF16), vm((8, WIDTH, 128), BF16), vm((WIDTH, 2 * WIDTH), BF16), vm((3, 16, 8, 128), F32),
            vm((3, 16, 128), F32), vm((WIDTH, 32), BF16), vm((16, WIDTH), BF16), vm((WIDTH, 2 * C), BF16),
            vm((WIDTH, 2 * WIDTH), BF16), vm((WIDTH, WIDTH), BF16), vm((WIDTH, 128), BF16), vm((WIDTH, 128), F32),
            vm((chunks, WIDTH, span), BF16), vm((chunks, 8 * 128, span), BF16),
            vm((chunks, 2 * WIDTH, span), BF16), vm((chunks, WIDTH, span), BF16), vm((chunks, WIDTH, span), F32),
            vm((chunks, WIDTH, span), BF16), vm((chunks, 2 * C, span), BF16), vm((chunks, WIDTH, span), F32),
            vm((chunks, C, span), BF16), vm((chunks, 8, span), F32), vm((chunks, 1, span), F32), vm((9 * C, WIDTH), F32),
            vm((9 * C, WIDTH), BF16),
            vm((96, WIDTH), F32), vm((8, 8, 128), F32), vm((8, 8, 128), F32),
            pltpu.SemaphoreType.DMA((15,)), pltpu.SemaphoreType.DMA((8,)), pltpu.SemaphoreType.DMA((8,)),
            pltpu.SemaphoreType.DMA((8,)), pltpu.SemaphoreType.DMA((8,)),
        ],
        compiler_params=pltpu.CompilerParams(collective_id=0, has_side_effects=True, vmem_limit_bytes=56 * 1024 * 1024),
        name="layer",
    )(
        rel_vec, atom_feat, centre.reshape(16, 128), nbr_slot.reshape(16, 128), edge_mask.reshape(16, 128), send_rows, w_radial,
        w_centre, w_nbr, w_env.T, w_val.T, w_mix, w_scal, w_read, w_out.reshape(1, WIDTH),
    )
    total = result[0] + result[1]
    return (total[3], total[0:3])


def solution(mesh):
    edges = P(("space", "grp"))
    placed = (
        P(None, ("space", "grp")), P(("space", "grp"), None), edges, edges, edges, P(("space", "grp"), None),
    ) + (P(),) * 9
    return jax.shard_map(
        functools.partial(per_device, mesh.shape["space"], mesh.shape["grp"]),
        mesh=mesh,
        in_specs=placed,
        out_specs=(edges, P(None, ("space", "grp"))),
        check_vma=False,
    )
```

time: 34.3 us -> 31 us (0.904)
  Pallas kernels: 31.7 us -> 29.6 us
  local copies, waits for them, and re-layouts: 1.79 us -> 0.59 us
    pallas_call x1, Pallas kernels: 31.7 us -> 29.6 us  [per_device(): pl.pallas_call(functools.partial(kernel, space, grp, span), out_shape=[vm...]
    unnamed x6 -> x2, local copies, waits for them, and re-layouts: 1.79 us -> 0.02 us
    slice x0 -> x1, local copies, waits for them, and re-layouts: none -> 0.57 us  [per_device(): return (total[3], total[0:3])]
where the time goes in v3:
time: 31 us; the launch traced here: 30.8 us
  Pallas kernels  29.6 us (95%)
  between operations  0.66 us (2%)
  local copies, waits for them, and re-layouts  0.59 us (2%)
    pallas_call x1, Pallas kernels, per_device(): pl.pallas_call(functools.partial(kernel, space, grp, span), out_shape=[vm...  29.6 us

profile of v3, /device:TPU:1, one launch (start us, length us, event | category | flops | bytes accessed | tf_op | source)
XLA Modules:
  0.0 30.8 jit_solution(4367006571767944968)
XLA Ops:
  0.6 29.6 %layer.1 = (f32[4,256]{1,0:T(4,128)S(1)}, f32[4,256]{1,0:T(4,128)S(1)}) custom-call(f32[3,2048]{1,0:T(4,128)} %vec_in.1, bf16[256,256]{1,0:T(8,128)(2,1)} %feat_in.1, s32[16,128]{1,0:T(8,128)} %bitcast.10, s32[16,128]{1,0:T(8,128)} %bitcast.11, s32[16,128]{1,0:T(8,128)} %bitcast.12, s32[1,128]{1,0:T(1,128)} %rows_in.1, f32[8,256]{1,0:T(8,128)} %w_radial_in.1, ...), custom_call_target="tpu_custom_call" | custom-call | tf_op jit(solution)/shard_map/layer/pallas_call | solution.py:385
  30.2 0.0 copy-start
  30.2 0.6 %slice.8 = f32[1,256]{1,0:T(1,128)} slice(f32[4,256]{1,0:T(4,128)S(1)} %add.3), slice={[3:4], [0:256]} | slice | bytes 2048 | tf_op jit(solution)/shard_map/slice | solution.py:414
  30.8 0.0 copy-done
  (1 shorter events, 0.0 us)
Async XLA Ops:
  30.2 0.6 %copy-start = (f32[4,256]{1,0:T(4,128)}, f32[4,256]{1,0:T(4,128)S(1)}, u32[]{:S(2)}) copy-start(f32[4,256]{1,0:T(4,128)S(1)} %add.3) | copy-start | bytes 12292

commit v4 on v3

--- a/solution.py
+++ b/solution.py
@@ -12,7 +12,8 @@
 BF16 = jnp.bfloat16
 MESH = pl.DeviceIdType.MESH
 OFFSETS = ((-1, -1), (-1, 0), (-1, 1), (0, -1), (0, 1), (1, -1), (1, 0), (1, 1))
-STAGES = ((0, 1), (2, 3), (4, 5, 6, 7))
+STAGES = ((0, 1, 2, 3), (4, 5, 6, 7))
+ORDER = (2, 3, 6, 7, 0, 1)
 BACK = (0, 1, 3, 2, 5, 4, 7, 6)
 CUTOFF = 5.0
 R3, R5, R15 = math.sqrt(3.0), math.sqrt(5.0), math.sqrt(15.0)
@@ -70,15 +71,11 @@
     return block if harm is None else block * harm
 
 
-def harmonics_exact(x, y, z):
+def harmonics(x, y, z):
     return [
         None, R3 * x, R3 * y, R3 * z,
         R15 * x * y, R15 * y * z, 0.5 * R5 * (3.0 * z * z - 1.0), R15 * x * z, 0.5 * R15 * (x * x - y * y),
     ]
-
-
-def harmonics(x, y, z):
-    return [None] + [harm.astype(BF16) for harm in harmonics_exact(x, y, z)[1:]]
 
 
 def geometry(vec, centre, slot, mask, geo, dense):
@@ -163,8 +160,8 @@
     def passed(role):
         return remote(tab.at[role - 2], tab.at[role], send_sem.at[role], recv_sem.at[role], partners[0])
 
-    copies = {role: sent(role) for role in (3, 2, 7, 6, 1, 0)}
-    for role in (3, 2, 7, 6, 1, 0):
+    copies = {role: sent(role) for role in ORDER}
+    for role in ORDER:
         copies[role].start()
     for load in loads[3:]:
         load.wait()
@@ -223,9 +220,8 @@
         copies[role + 2].start()
     for role in (0, 1):
         copies[role].wait_recv()
-    for stage in STAGES[:2]:
-        for j in range(chunks):
-            act_s[j] = gathered(j, stage)
+    for j in range(chunks):
+        act_s[j] = gathered(j, STAGES[0])
     for role in (4, 5):
         copies[role].wait_recv()
     for role in (6, 7):
@@ -233,7 +229,7 @@
 
     def forward(j):
         x, y, z, _, envelope, _, _, _ = fields(j)
-        lifted = gathered(j, STAGES[2])
+        lifted = gathered(j, STAGES[1])
         yield
         active, slope = gated(lifted)
         actb_s[j] = active.astype(BF16)
@@ -241,19 +237,19 @@
         latent = (active * envelope).astype(BF16)
         lat_s[j, 0:WIDTH] = latent
         yield
-        wv = mm(wevt[...], latent).astype(BF16)
-        wv_s[j] = wv
+        wv = mm(wevt[...], latent)
+        wv_s[j] = wv.astype(BF16)
         yield
         weights = wv[:C]
         harm = harmonics(x, y, z)
-        spread = jnp.concatenate([scaled(weights, harm[i]) for i in range(9)], axis=0)
+        spread = jnp.concatenate([scaled(weights, harm[i]).astype(BF16) for i in range(9)], axis=0)
         yield
         add(env_s, mm_nt(spread, hot_s[j]), j)
 
     def middle(j):
         x, y, z, _, _, _, _, _ = fields(j)
         hot = hot_s[j]
-        exact, harm = harmonics_exact(x, y, z), harmonics(x, y, z)
+        harm = harmonics(x, y, z)
         local = mm(envh_s[...], hot)
         yield
         values = wv_s[j, C:]
@@ -261,7 +257,7 @@
         for degree in DEGREES:
             whole = None
             for i in degree:
-                term = scaled(part(local, i), exact[i])
+                term = scaled(part(local, i), harm[i])
                 whole = term if whole is None else whole + term
             invariants.append(whole.astype(BF16))
         lat_s[j, WIDTH:] = jnp.concatenate([q * values for q in invariants] + [jnp.zeros_like(values)], axis=0)
@@ -292,12 +288,11 @@
             bar = part(scal_bar, level)
             term = bar * invariants[level]
             values_bar = term if values_bar is None else values_bar + term
-            inner_f = part(scal_f, level) * values.astype(F32)
-            inner = inner_f.astype(BF16)
+            inner = part(scal_f, level) * values.astype(F32)
             for i in degree:
-                locals_bar.append(scaled(inner, harm[i]))
+                locals_bar.append(scaled(inner, harm[i]).astype(BF16))
                 if i:
-                    products.append(down(part(local, i) * inner_f))
+                    products.append(down(part(local, i) * inner))
         vbar_s[j] = values_bar
         hbar_s[j] = jnp.concatenate(products, axis=0)
         yield
@@ -307,7 +302,7 @@
         x, y, z, inv, envelope, slope_env, centres, slots = fields(j)
         slots, centres = index(slots), index(centres)
         hot = hot_s[j]
-        harm = harmonics_exact(x, y, z)
+        harm = harmonics(x, y, z)
         spread_bar = mm(envh_s[...], hot)
         yield
         weights = wv_s[j, :C].astype(F32)

time: 31 us -> 30.5 us (0.984)
  Pallas kernels: 29.6 us -> 29.1 us
    pallas_call x1, Pallas kernels: 29.6 us -> 29.1 us  [per_device(): pl.pallas_call(functools.partial(kernel, space, grp, span), out_shape=[vm...]
where the time goes in v4:
time: 30.5 us; the launch traced here: 30.3 us
  Pallas kernels  29.1 us (95%)
  between operations  0.66 us (2%)
  local copies, waits for them, and re-layouts  0.59 us (2%)
    pallas_call x1, Pallas kernels, per_device(): pl.pallas_call(functools.partial(kernel, space, grp, span), out_shape=[vm...  29.1 us

profile of v4, /device:TPU:1, one launch (start us, length us, event | category | flops | bytes accessed | tf_op | source)
XLA Modules:
  0.0 30.3 jit_solution(10673643931565057829)
XLA Ops:
  0.6 29.1 %layer.1 = (f32[4,256]{1,0:T(4,128)S(1)}, f32[4,256]{1,0:T(4,128)S(1)}) custom-call(f32[3,2048]{1,0:T(4,128)} %vec_in.1, bf16[256,256]{1,0:T(8,128)(2,1)} %feat_in.1, s32[16,128]{1,0:T(8,128)} %bitcast.10, s32[16,128]{1,0:T(8,128)} %bitcast.11, s32[16,128]{1,0:T(8,128)} %bitcast.12, s32[1,128]{1,0:T(1,128)} %rows_in.1, f32[8,256]{1,0:T(8,128)} %w_radial_in.1, ...), custom_call_target="tpu_custom_call" | custom-call | tf_op jit(solution)/shard_map/layer/pallas_call | solution.py:380
  29.8 0.0 copy-start
  29.8 0.6 %slice.8 = f32[1,256]{1,0:T(1,128)} slice(f32[4,256]{1,0:T(4,128)S(1)} %add.3), slice={[3:4], [0:256]} | slice | bytes 2048 | tf_op jit(solution)/shard_map/slice | solution.py:409
  30.3 0.0 copy-done
  (1 shorter events, 0.0 us)
Async XLA Ops:
  29.8 0.6 %copy-start = (f32[4,256]{1,0:T(4,128)}, f32[4,256]{1,0:T(4,128)S(1)}, u32[]{:S(2)}) copy-start(f32[4,256]{1,0:T(4,128)S(1)} %add.3) | copy-start | bytes 12292

commit v5 on v4

--- a/solution.py
+++ b/solution.py
@@ -38,7 +38,7 @@
 def gated(half):
     rise = 1.0 + jnp.tanh(half)
     active = half * rise
-    return active, (rise + active * (2.0 - rise)).astype(BF16)
+    return active, rise + active * (2.0 - rise)
 
 
 def halved(block):
@@ -238,7 +238,7 @@
         lat_s[j, 0:WIDTH] = latent
         yield
         wv = mm(wevt[...], latent)
-        wv_s[j] = wv.astype(BF16)
+        wv_s[j] = wv
         yield
         weights = wv[:C]
         harm = harmonics(x, y, z)
@@ -259,28 +259,27 @@
             for i in degree:
                 term = scaled(part(local, i), harm[i])
                 whole = term if whole is None else whole + term
-            invariants.append(whole.astype(BF16))
-        lat_s[j, WIDTH:] = jnp.concatenate([q * values for q in invariants] + [jnp.zeros_like(values)], axis=0)
+            invariants.append(whole)
+        lat_s[j, WIDTH:] = jnp.concatenate([(q * values).astype(BF16) for q in invariants] + [jnp.zeros((C, span), BF16)], axis=0)
         yield
         update = mm(wmixt[...], lat_s[j])
         yield
         active, slope = gated(update)
-        mixed = lat_s[j, 0:WIDTH] + active.astype(BF16)
+        mixed = (lat_s[j, 0:WIDTH].astype(F32) + active).astype(BF16)
         yield
         hidden = mm(wreadt[...], mixed)
         yield
         active_h, slope_h = gated(hidden)
         en_s[j] = down(active_h * jnp.concatenate([woutf[...]] * wide, axis=1))
-        hidden_bar = jnp.concatenate([wout[...]] * wide, axis=1) * slope_h
+        hidden_bar = jnp.concatenate([wout[...]] * wide, axis=1) * slope_h.astype(BF16)
         yield
         mixed_bar = mm(w_read[...], hidden_bar)
         yield
         mixed_bar = mixed_bar.astype(BF16)
-        update_bar = mixed_bar * slope
+        update_bar = mixed_bar * slope.astype(BF16)
         yield
         back_s[j] = mixed_bar.astype(F32) + mm(w_mix[...], update_bar)
-        scal_f = mm(w_scal[...], update_bar)
-        scal_bar = scal_f.astype(BF16)
+        scal_bar = mm(w_scal[...], update_bar)
         yield
         values_bar = None
         locals_bar, products = [], []
@@ -288,12 +287,12 @@
             bar = part(scal_bar, level)
             term = bar * invariants[level]
             values_bar = term if values_bar is None else values_bar + term
-            inner = part(scal_f, level) * values.astype(F32)
+            inner = bar * values
             for i in degree:
                 locals_bar.append(scaled(inner, harm[i]).astype(BF16))
                 if i:
                     products.append(down(part(local, i) * inner))
-        vbar_s[j] = values_bar
+        vbar_s[j] = values_bar.astype(BF16)
         hbar_s[j] = jnp.concatenate(products, axis=0)
         yield
         add(env_s, mm_nt(jnp.concatenate(locals_bar, axis=0), hot), j)
@@ -305,20 +304,19 @@
         harm = harmonics(x, y, z)
         spread_bar = mm(envh_s[...], hot)
         yield
-        weights = wv_s[j, :C].astype(F32)
+        weights = wv_s[j, :C]
         weights_bar = part(spread_bar, 0)
         for i in range(1, 9):
             weights_bar = weights_bar + part(spread_bar, i) * harm[i]
         products = [down(part(spread_bar, i) * weights) for i in range(1, 9)]
         wv_bar = jnp.concatenate([weights_bar.astype(BF16), vbar_s[j]], axis=0)
         yield
-        latent_f = back_s[j] + mm(wev[...], wv_bar)
-        latent_bar = latent_f.astype(BF16)
+        latent_bar = back_s[j] + mm(wev[...], wv_bar)
         harm_bar = hbar_s[j] + jnp.concatenate(products, axis=0)
         bars = [None] + [harm_bar[i : i + 1] for i in range(8)]
         yield
-        envelope_bar = down(latent_f * actb_s[j].astype(F32))
-        lifted_bar = latent_bar * envelope.astype(BF16) * slope_s[j]
+        envelope_bar = down(latent_bar * actb_s[j].astype(F32))
+        lifted_bar = (latent_bar * envelope * slope_s[j]).astype(BF16)
         yield
         radial_bar = mm(wrhl[...], lifted_bar)
         yield
@@ -392,7 +390,7 @@
             vm((WIDTH, 2 * WIDTH), BF16), vm((WIDTH, WIDTH), BF16), vm((WIDTH, 128), BF16), vm((WIDTH, 128), F32),
             vm((chunks, WIDTH, span), BF16), vm((chunks, 8 * 128, span), BF16),
             vm((chunks, 2 * WIDTH, span), BF16), vm((chunks, WIDTH, span), BF16), vm((chunks, WIDTH, span), F32),
-            vm((chunks, WIDTH, span), BF16), vm((chunks, 2 * C, span), BF16), vm((chunks, WIDTH, span), F32),
+            vm((chunks, WIDTH, span), F32), vm((chunks, 2 * C, span), F32), vm((chunks, WIDTH, span), F32),
             vm((chunks, C, span), BF16), vm((chunks, 8, span), F32), vm((chunks, 1, span), F32), vm((9 * C, WIDTH), F32),
             vm((9 * C, WIDTH), BF16),
             vm((96, WIDTH), F32), vm((8, 8, 128), F32), vm((8, 8, 128), F32),

time: 30.5 us -> 30.5 us (level)
  no operation moved by 1% of the time
where the time goes in v5:
time: 30.5 us; the launch traced here: 30.4 us
  Pallas kernels  29.1 us (95%)
  between operations  0.66 us (2%)
  local copies, waits for them, and re-layouts  0.59 us (2%)
    pallas_call x1, Pallas kernels, per_device(): pl.pallas_call(functools.partial(kernel, space, grp, span), out_shape=[vm...  29.1 us

profile of v5, /device:TPU:1, one launch (start us, length us, event | category | flops | bytes accessed | tf_op | source)
XLA Modules:
  0.0 30.4 jit_solution(6655691315954714726)
XLA Ops:
  0.6 29.1 %layer.1 = (f32[4,256]{1,0:T(4,128)S(1)}, f32[4,256]{1,0:T(4,128)S(1)}) custom-call(f32[3,2048]{1,0:T(4,128)} %vec_in.1, bf16[256,256]{1,0:T(8,128)(2,1)} %feat_in.1, s32[16,128]{1,0:T(8,128)} %bitcast.10, s32[16,128]{1,0:T(8,128)} %bitcast.11, s32[16,128]{1,0:T(8,128)} %bitcast.12, s32[1,128]{1,0:T(1,128)} %rows_in.1, f32[8,256]{1,0:T(8,128)} %w_radial_in.1, ...), custom_call_target="tpu_custom_call" | custom-call | tf_op jit(solution)/shard_map/layer/pallas_call | solution.py:378
  29.8 0.0 copy-start
  29.8 0.6 %slice.8 = f32[1,256]{1,0:T(1,128)} slice(f32[4,256]{1,0:T(4,128)S(1)} %add.3), slice={[3:4], [0:256]} | slice | bytes 2048 | tf_op jit(solution)/shard_map/slice | solution.py:407
  30.4 0.0 copy-done
  (1 shorter events, 0.0 us)
Async XLA Ops:
  29.8 0.6 %copy-start = (f32[4,256]{1,0:T(4,128)}, f32[4,256]{1,0:T(4,128)S(1)}, u32[]{:S(2)}) copy-start(f32[4,256]{1,0:T(4,128)S(1)} %add.3) | copy-start | bytes 12292
